TPU v7x, 32 devices: a whole 2x2x4 slice. The times are simulated.
32 devices in a mesh: basis: 16 (over z, y, core), state: 2 (over x).
Axes of the slice: x: 2, y: 2, z: 4, core: 2. Of those that a mesh axis runs over, the one named last changes fastest.
Arguments:
- vectors: bfloat16 [512, 81920], P('state', 'basis'), may hold values from -6 to 6
- blocks: bfloat16 [640, 18, 128, 128], P('basis', 'state'), may hold values from -0.125 to 0.125
- columns: int32 [640, 18], P('basis', 'state'), may hold values from 0 to 639, as said below
- counts: int32 [640], P('basis'), may hold values from 4 to 18, as said below
Outputs:
- sigma: bfloat16 [512, 81920], P('state', 'basis')
Inputs may be any that keep to these rules, and one draw needn't show every extreme that they name: Every block column lies within 36 blocks of its block row and inside the basis; a row's slots name distinct columns except near the basis ends, where a column may repeat. Slots k < counts[r] are live; some block row has all 18 slots live.
All inputs are finite; a program needn't handle non-finite values.
Results may differ from a plain program's by a relative error of at most 0.001.
Values may be sent and summed in bfloat16 or wider, within the bound.
No kernel may reach another device: no remote copies, remote signals or barrier semaphores. Data moves between devices by JAX's collectives and lax.ppermute only.
A program may use at most 192 MiB of HBM per device.

v0:
```python
import functools
import math

import jax
import jax.numpy as jnp
from jax import lax
from jax.experimental import pallas as pl
from jax.experimental.pallas import tpu as pltpu
from jax.sharding import PartitionSpec as P

W = 36
VMEM_LIMIT = 32 * 1024 * 1024
TOP = 32767.0
FINE = 65536.0
SMALLEST = 2.0**-100


def after(array, *others):
    return lax.optimization_barrier((array, *others))[0]


def fill(sources, plan, ext, sems):
    copies, at = [], 0
    for part, (start, size, _) in enumerate(plan):
        left, own, right = sources[3 * part : 3 * part + 3]
        reach, width = left.shape[1], own.shape[1]
        rows = pl.ds(at, size)
        copies += [
            pltpu.make_async_copy(left, ext.at[rows, pl.ds(0, reach)], sems.at[3 * part]),
            pltpu.make_async_copy(
                own.at[pl.ds(start, size)], ext.at[rows, pl.ds(reach, width)], sems.at[3 * part + 1]
            ),
            pltpu.make_async_copy(right, ext.at[rows, pl.ds(reach + width, reach)], sems.at[3 * part + 2]),
        ]
        at += size
    for copy in copies:
        copy.start()
    return copies


def row_sums(index_ref, row, slots, block, ext, panel_ref):
    picked = jnp.concatenate(
        [
            ext[:, pl.ds(pl.multiple_of(index_ref[row * slots + slot] * block, block), block)]
            for slot in range(slots)
        ],
        axis=1,
    )
    panel = jnp.concatenate([panel_ref[slot] for slot in range(slots)], axis=1)
    return lax.dot_general(
        picked, panel, (((1,), (1,)), ((), ())), preferred_element_type=jnp.float32
    )


def level_code(top):
    return jnp.ceil(jnp.log2(jnp.maximum(top, SMALLEST)) * FINE).astype(jnp.int32)


def level_of(code):
    return jnp.exp2(code.astype(jnp.float32) * (1.0 / FINE))


def code_into(out_ref, first, block, words, sums):
    lane = lax.broadcasted_iota(jnp.int32, (out_ref.shape[0], block), 1)
    codes = out_ref[:, words * block :]
    values = []
    for member, mine in enumerate(sums):
        code = level_code(jnp.max(jnp.abs(mine), axis=1, keepdims=True))
        codes = jnp.where(lane == first + member, code, codes)
        scaled = jnp.round(mine * (TOP / level_of(code)))
        values.append(jnp.clip(scaled, -TOP, TOP).astype(jnp.int32))
    out_ref[:, words * block :] = codes
    for pair in range(len(sums) // 2):
        word = (values[2 * pair + 1] << 16) | (values[2 * pair] & 0xFFFF)
        at = pl.multiple_of((first // 2 + pair) * block, block)
        out_ref[:, pl.ds(at, block)] = word


def products_kernel(plan, group, slots, block, words, index_ref, *refs):
    parts = len(plan)
    sources, blocks_ref = refs[: 3 * parts], refs[3 * parts]
    outs, (ext, panels, sems, panel_sems) = refs[3 * parts + 1 : 4 * parts + 1], refs[4 * parts + 1 :]
    rows, pieces = panels.shape[0], panel_sems.shape[0]
    piece = rows // pieces

    def panel_copy(n):
        here = pl.ds(n * piece, piece)
        return pltpu.make_async_copy(blocks_ref.at[here], panels.at[here], panel_sems.at[n])

    copies = fill(sources, plan, ext, sems)
    for n in range(pieces):
        panel_copy(n).start()
    end = ext.shape[1] - block
    ext[:, end:] = jnp.zeros((ext.shape[0], block), ext.dtype)
    for (_, size, coded), out_ref in zip(plan, outs):
        if coded:
            out_ref[:, words * block :] = jnp.zeros((size, block), jnp.int32)
    for copy in copies:
        copy.wait()

    @pl.loop(0, rows // group)
    def _(step):
        for n in range(group // piece):
            panel_copy(step * (group // piece) + n).wait()
        first = step * group
        sums = [
            row_sums(index_ref, first + member, slots, block, ext, panels.at[first + member])
            for member in range(group)
        ]
        at = 0
        for (_, size, coded), out_ref in zip(plan, outs):
            mine = [total[at : at + size] for total in sums]
            if coded:
                code_into(out_ref, first, block, words, mine)
            else:
                for member in range(group):
                    column = pl.multiple_of((first + member) * block, block)
                    out_ref[:, pl.ds(column, block)] = mine[member]
            at += size


def products(index, parts, blocks):
    rows, slots, block, _ = blocks.shape
    reach, width = parts[0][0].shape[1], parts[0][1].shape[1]
    plan = tuple(part[3:] for part in parts)
    states = sum(size for _, size, _ in plan)
    group, words = 8 if rows % 8 == 0 else 2, rows // 2
    sources = [array for part in parts for array in part[:3]]
    anywhere = pl.BlockSpec(memory_space=pl.ANY)
    out_shape = []
    for _, size, coded in plan:
        if coded:
            out_shape.append(jax.ShapeDtypeStruct((size, (words + 1) * block), jnp.int32))
        else:
            out_shape.append(jax.ShapeDtypeStruct((size, width), jnp.float32))
    return pl.pallas_call(
        functools.partial(products_kernel, plan, group, slots, block, words),
        out_shape=out_shape,
        in_specs=[pl.BlockSpec(memory_space=pltpu.SMEM)]
        + [anywhere] * len(sources)
        + [pl.BlockSpec(memory_space=pltpu.HBM)],
        out_specs=[pl.BlockSpec(memory_space=pltpu.VMEM)] * len(plan),
        scratch_shapes=[
            pltpu.VMEM((states, 2 * reach + width + block), parts[0][1].dtype),
            pltpu.VMEM(blocks.shape, blocks.dtype),
            pltpu.SemaphoreType.DMA((len(sources),)),
            pltpu.SemaphoreType.DMA((rows // 2,)),
        ],
        compiler_params=pltpu.CompilerParams(vmem_limit_bytes=VMEM_LIMIT),
        cost_estimate=pl.CostEstimate(flops=1, bytes_accessed=1, transcendentals=0),
        name="products",
    )(index, *sources, pltpu.with_memory_space_constraint(blocks, pltpu.HBM))


def finish_kernel(partials, block, pairs, own_ref, *refs):
    out_ref = refs[-1]
    step = pl.program_id(0)
    lane = lax.broadcasted_iota(jnp.int32, (own_ref.shape[0], block), 1)
    levels = [level_of(refs[2 * p + 1][...]) * (1.0 / TOP) for p in range(partials)]
    for pair in range(pairs):
        for half in range(2):
            at = (2 * pair + half) * block
            row = (step * pairs + pair) * 2 + half
            total = own_ref[:, at : at + block]
            for p in range(partials):
                word = refs[2 * p][:, pair * block : (pair + 1) * block]
                value = (word >> 16) if half else ((word << 16) >> 16)
                level = jnp.max(jnp.where(lane == row, levels[p], 0.0), axis=1, keepdims=True)
                total = total + value.astype(jnp.float32) * level
            out_ref[:, at : at + block] = total.astype(out_ref.dtype)


def finish(own_sums, own_start, coded, coded_start, out, start, size, states, block):
    width = own_sums.shape[1]
    words = width // block // 2
    pairs = words // 2 if words % 2 == 0 else 1
    rows, wide, narrow = pl.Element(size), pl.Element(2 * pairs * block), pl.Element(pairs * block)
    own_at, coded_at = start - own_start, start - coded_start
    in_specs = [pl.BlockSpec((rows, wide), lambda i: (own_at, i * 2 * pairs * block))]
    operands = [own_sums]
    for array in coded:
        in_specs.append(pl.BlockSpec((rows, narrow), lambda i: (coded_at, i * pairs * block)))
        in_specs.append(pl.BlockSpec((rows, pl.Element(block)), lambda i: (coded_at, words * block)))
        operands += [array, array]
    aliases = {}
    if out is not None:
        aliases = {len(operands): 0}
        in_specs.append(pl.BlockSpec(memory_space=pl.ANY))
        operands.append(out)
    return pl.pallas_call(
        functools.partial(finish_kernel, len(coded), block, pairs),
        out_shape=jax.ShapeDtypeStruct((states, width), jnp.bfloat16),
        grid=(words // pairs,),
        in_specs=in_specs,
        out_specs=pl.BlockSpec((rows, wide), lambda i: (start, i * 2 * pairs * block)),
        input_output_aliases=aliases,
        compiler_params=pltpu.CompilerParams(vmem_limit_bytes=VMEM_LIMIT),
        cost_estimate=pl.CostEstimate(flops=1, bytes_accessed=1, transcendentals=0),
        name="finish",
    )(*operands)


def starts_of(sizes):
    return [sum(sizes[:i]) for i in range(len(sizes))]


def on_device(vectors, blocks, columns, counts):
    states, width = vectors.shape
    rows, slots, block, _ = blocks.shape
    reach = W * block
    basis_size, state_size = lax.axis_size("basis"), lax.axis_size("state")
    if states % 256 == 0:
        sizes = (5 * states // 16, 5 * states // 16, 3 * states // 8)
        own_sizes = (3 * states // 8, 5 * states // 8)
    else:
        sizes, own_sizes = (states,), (states,)
    starts, own_starts = starts_of(sizes), starts_of(own_sizes)

    slot_index = lax.axis_index("state") * slots + jnp.arange(slots, dtype=jnp.int32)
    relative = columns - (lax.axis_index("basis") * rows - W)
    zeros_at = rows + 2 * W
    index = jnp.where(slot_index[None, :] < counts[:, None], relative, zeros_at).reshape(-1)

    up = [(i, i + 1) for i in range(basis_size - 1)]
    down = [(i + 1, i) for i in range(basis_size - 1)]

    def edges_of(piece, *others):
        edges = (piece[:, width - reach :], piece[:, :reach])
        return lax.optimization_barrier((*edges, *others))[:2] if others else edges

    def halo(edges):
        return lax.ppermute(edges[0], "basis", up), lax.ppermute(edges[1], "basis", down)

    def shifted(piece, shift):
        return lax.ppermute(piece, "state", [(i, (i + shift) % state_size) for i in range(state_size)])

    def own_edges(part, *others):
        return edges_of(vectors[own_starts[part] : own_starts[part] + own_sizes[part]], *others)

    def own_part(part, ends):
        return (ends[0], vectors, ends[1], own_starts[part], own_sizes[part], False)

    def their_part(n):
        return (ends[n][0], theirs[n], ends[n][1], 0, theirs[n].shape[0], True)

    messages = [(shift, c) for shift in range(1, state_size) for c in range(len(sizes))]
    count = len(messages)
    theirs, edges, ends, sent, own_sums, received = [], [], [], [], [], []
    first_edges = own_edges(0)
    first = halo(first_edges)
    for n, (shift, c) in enumerate(messages):
        source = after(vectors, *(first_edges if n == 1 else first)) if n else vectors
        theirs.append(shifted(source[starts[c] : starts[c] + sizes[c]], shift))

    def compute(n):
        later = edges[n + 1] if n + 1 < len(edges) else ()
        sent.extend(products(after(index, *later) if later else index, [their_part(n)], blocks))
        message = after(sent[n], received[n - 1]) if n else sent[n]
        received.append(shifted(message, -messages[n][0]))

    for n in range(count):
        edges.append(edges_of(theirs[n]))
        ends.append(halo(edges[n]))
        if n:
            compute(n - 1)
    if len(own_sizes) > 1:
        edges.append(own_edges(1, *edges[-1], *sent[-1:], *received[:1]))
        last = halo(edges[-1])
    compute(count - 1)
    coded = [[received[n] for n in range(count) if messages[n][1] == c] for c in range(len(sizes))]
    own_sums += products(after(index, sent[-1]), [own_part(0, first)], blocks)
    out = None
    for part, own_size in enumerate(own_sizes):
        if part:
            own_sums += products(after(index, out), [own_part(part, last)], blocks)
        for c, size in enumerate(sizes):
            at = max(own_starts[part], starts[c])
            end = min(own_starts[part] + own_size, starts[c] + size)
            if at < end:
                out = finish(
                    own_sums[part], own_starts[part], coded[c], starts[c], out, at, end - at, states, block
                )
    return out


def solution(mesh):
    in_specs = (
        P("state", "basis"),
        P("basis", "state", None, None),
        P("basis", "state"),
        P("basis"),
    )
    out_specs = P("state", "basis")
    return jax.shard_map(
        on_device, mesh=mesh, in_specs=in_specs, out_specs=out_specs, check_vma=False
    )
```

profile of v0, /device:TPU:9, one launch (start us, length us, event | category | flops | bytes accessed | tf_op | source)
XLA Modules:
  0.0 136.8 jit_solution(5067567919464682608)
XLA Ops:
  0.0 2.2 %slice.55 = bf16[80,5120]{1,0:T(8,128)(2,1)} slice(bf16[256,5120]{1,0:T(8,128)(2,1)} %refs_1_.3), slice={[0:80], [0:5120]} | slice | bytes 1638400 | tf_op jit(solution)/shard_map/slice | solution.py:253
  3.4 2.8 %fusion = (bf16[96,4608]{1,0:T(8,128)(2,1)}, bf16[96,4608]{1,0:T(8,128)(2,1)}) fusion(bf16[256,5120]{1,0:T(8,128)(2,1)} %refs_1_.3), kind=kLoop, calls=%fused_computation.2 | loop fusion | bytes 3538944 | tf_op jit(solution)/shard_map/slice | solution.py:228
  6.2 2.9 %collective-permute-start.1 = (bf16[96,4608]{1,0:T(8,128)(2,1)}, bf16[96,4608]{1,0:T(8,128)(2,1)}, u32[]{:S(2)}, u32[]{:S(2)}) collective-permute-start(bf16[96,4608]{1,0:T(8,128)(2,1)} %get-tuple-element.27), channel_id=1, source_target_pairs={{2,0},{4,2},{6,4},{8,6},{10,8},{12,10},{14,12},{16,14},{18,16},{20... | collective-permute-start | bytes 2654216 | tf_op jit(solution)/shard_map/ppermute | solution.py:232
  9.1 3.0 %collective-permute-start = (bf16[96,4608]{1,0:T(8,128)(2,1)}, bf16[96,4608]{1,0:T(8,128)(2,1)}, u32[]{:S(2)}, u32[]{:S(2)}) collective-permute-start(bf16[96,4608]{1,0:T(8,128)(2,1)} %get-tuple-element.28), channel_id=1, source_target_pairs={{0,2},{2,4},{4,6},{6,8},{8,10},{10,12},{12,14},{14,16},{16,18},{18... | collective-permute-start | bytes 2654216 | tf_op jit(solution)/shard_map/ppermute | solution.py:232
  13.7 8.0 %collective-permute-done.6.refs_1_ = bf16[80,5120]{1,0:T(8,128)(2,1)} collective-permute-done((bf16[80,5120]{1,0:T(8,128)(2,1)}, bf16[80,5120]{1,0:T(8,128)(2,1)}, u32[]{:S(2)}, u32[]{:S(2)}) %collective-permute-start.6) | collective-permute-done | bytes 819232 | tf_op jit(solution)/shard_map/ppermute | solution.py:235
  23.1 4.6 %collective-permute-start.8 = (bf16[80,4608]{1,0:T(8,128)(2,1)S(1)}, bf16[80,4608]{1,0:T(8,128)(2,1)S(1)}, u32[]{:S(2)}, u32[]{:S(2)}) collective-permute-start(bf16[80,4608]{1,0:T(8,128)(2,1)S(1)} %get-tuple-element.33), channel_id=1, source_target_pairs={{2,0},{4,2},{6,4},{8,6},{10,8},{12,10},{14,12},{16,14},{18,16},{20... | collective-permute-start | bytes 2211848 | tf_op jit(solution)/shard_map/ppermute | solution.py:232
  27.8 3.0 %collective-permute-start.7 = (bf16[80,4608]{1,0:T(8,128)(2,1)S(1)}, bf16[80,4608]{1,0:T(8,128)(2,1)S(1)}, u32[]{:S(2)}, u32[]{:S(2)}) collective-permute-start(bf16[80,4608]{1,0:T(8,128)(2,1)S(1)} %get-tuple-element.34), channel_id=1, source_target_pairs={{0,2},{2,4},{4,6},{6,8},{8,10},{10,12},{12,14},{14,16},{16,18},{18... | collective-permute-start | bytes 2211848 | tf_op jit(solution)/shard_map/ppermute | solution.py:232
  30.9 7.6 %collective-permute-done.refs_0_ = bf16[96,4608]{1,0:T(8,128)(2,1)} collective-permute-done((bf16[96,4608]{1,0:T(8,128)(2,1)}, bf16[96,4608]{1,0:T(8,128)(2,1)}, u32[]{:S(2)}, u32[]{:S(2)}) %collective-permute-start) | collective-permute-done | bytes 884768 | tf_op jit(solution)/shard_map/ppermute | solution.py:232
  39.2 3.5 %collective-permute-start.5 = (bf16[80,4608]{1,0:T(8,128)(2,1)S(1)}, bf16[80,4608]{1,0:T(8,128)(2,1)S(1)}, u32[]{:S(2)}, u32[]{:S(2)}) collective-permute-start(bf16[80,4608]{1,0:T(8,128)(2,1)S(1)} %get-tuple-element.35), channel_id=1, source_target_pairs={{2,0},{4,2},{6,4},{8,6},{10,8},{12,10},{14,12},{16,14},{18,16},{20... | collective-permute-start | bytes 2211848 | tf_op jit(solution)/shard_map/ppermute | solution.py:232
  42.7 4.2 %collective-permute-start.4 = (bf16[80,4608]{1,0:T(8,128)(2,1)S(1)}, bf16[80,4608]{1,0:T(8,128)(2,1)S(1)}, u32[]{:S(2)}, u32[]{:S(2)}) collective-permute-start(bf16[80,4608]{1,0:T(8,128)(2,1)S(1)} %get-tuple-element.36), channel_id=1, source_target_pairs={{0,2},{2,4},{4,6},{6,8},{8,10},{10,12},{12,14},{14,16},{16,18},{18... | collective-permute-start | bytes 2211848 | tf_op jit(solution)/shard_map/ppermute | solution.py:232
  46.9 7.3 %collective-permute-done.7.refs_0_ = bf16[80,4608]{1,0:T(8,128)(2,1)S(1)} collective-permute-done((bf16[80,4608]{1,0:T(8,128)(2,1)S(1)}, bf16[80,4608]{1,0:T(8,128)(2,1)S(1)}, u32[]{:S(2)}, u32[]{:S(2)}) %collective-permute-start.7) | collective-permute-done | bytes 737312 | tf_op jit(solution)/shard_map/ppermute | solution.py:232
  54.2 8.5 %products.6 = s32[80,2688]{1,0:T(8,128)S(1)} custom-call(s32[360]{0:T(512)S(1)} %reshape.8.index_ref, bf16[80,4608]{1,0:T(8,128)(2,1)S(1)} %collective-permute-done.7.refs_0_, bf16[80,5120]{1,0:T(8,128)(2,1)} %collective-permute-done.6.refs_1_, bf16[80,4608]{1,0:T(8,128)(2,1)S(1)} %collective-permute-done.8.refs_2_, bf16[40,9,128,128]{3,2,1,0:T(8,128)(2,1)} %refs_3_.9), custom_call_target="tpu_custom_call" | custom-call | flops 1 | bytes 1 | tf_op jit(solution)/shard_map/products/pallas_call | solution.py:136
  63.1 1.9 %collective-permute-start.11 = (bf16[96,4608]{1,0:T(8,128)(2,1)S(1)}, bf16[96,4608]{1,0:T(8,128)(2,1)S(1)}, u32[]{:S(2)}, u32[]{:S(2)}) collective-permute-start(bf16[96,4608]{1,0:T(8,128)(2,1)S(1)} %get-tuple-element.31), channel_id=1, source_target_pairs={{2,0},{4,2},{6,4},{8,6},{10,8},{12,10},{14,12},{16,14},{18,16},{20... | collective-permute-start | bytes 2654216 | tf_op jit(solution)/shard_map/ppermute | solution.py:232
  65.0 4.7 %collective-permute-start.10 = (bf16[96,4608]{1,0:T(8,128)(2,1)S(1)}, bf16[96,4608]{1,0:T(8,128)(2,1)S(1)}, u32[]{:S(2)}, u32[]{:S(2)}) collective-permute-start(bf16[96,4608]{1,0:T(8,128)(2,1)S(1)} %get-tuple-element.32), channel_id=1, source_target_pairs={{0,2},{2,4},{4,6},{6,8},{8,10},{10,12},{12,14},{14,16},{16,18},{18... | collective-permute-start | bytes 2654216 | tf_op jit(solution)/shard_map/ppermute | solution.py:232
  69.8 8.3 %products.5 = s32[80,2688]{1,0:T(8,128)S(1)} custom-call(s32[360]{0:T(512)S(1)} %reshape.8.index_ref, bf16[80,4608]{1,0:T(8,128)(2,1)S(1)} %collective-permute-done.4.refs_0_, bf16[80,5120]{1,0:T(8,128)(2,1)S(1)} %collective-permute-done.3.refs_1_, bf16[80,4608]{1,0:T(8,128)(2,1)S(1)} %collective-permute-done.5.refs_2_, bf16[40,9,128,128]{3,2,1,0:T(8,128)(2,1)} %refs_3_.9), custom_call_target="tpu_custom_call" | custom-call | flops 1 | bytes 1 | tf_op jit(solution)/shard_map/products/pallas_call | solution.py:136
  78.1 1.8 %collective-permute-done.9.refs_0_.refs_1_ = s32[80,2688]{1,0:T(8,128)S(1)} collective-permute-done((s32[80,2688]{1,0:T(8,128)S(1)}, s32[80,2688]{1,0:T(8,128)S(1)}, u32[]{:S(2)}, u32[]{:S(2)}) %collective-permute-start.9) | collective-permute-done | bytes 860192 | tf_op jit(solution)/shard_map/ppermute | solution.py:235
  81.2 3.7 %collective-permute-start.13 = (bf16[160,4608]{1,0:T(8,128)(2,1)S(1)}, bf16[160,4608]{1,0:T(8,128)(2,1)S(1)}, u32[]{:S(2)}, u32[]{:S(2)}) collective-permute-start(bf16[160,4608]{1,0:T(8,128)(2,1)S(1)} %get-tuple-element.20), channel_id=1, source_target_pairs={{0,2},{2,4},{4,6},{6,8},{8,10},{10,12},{12,14},{14,16},{16,18},{18... | collective-permute-start | bytes 4423688 | tf_op jit(solution)/shard_map/ppermute | solution.py:232
  84.9 1.9 %collective-permute-start.14 = (bf16[160,4608]{1,0:T(8,128)(2,1)S(1)}, bf16[160,4608]{1,0:T(8,128)(2,1)S(1)}, u32[]{:S(2)}, u32[]{:S(2)}) collective-permute-start(bf16[160,4608]{1,0:T(8,128)(2,1)S(1)} %get-tuple-element.21), channel_id=1, source_target_pairs={{2,0},{4,2},{6,4},{8,6},{10,8},{12,10},{14,12},{16,14},{18,16},{20... | collective-permute-start | bytes 4423688 | tf_op jit(solution)/shard_map/ppermute | solution.py:232
  86.8 17.3 %collective-permute-done.11.refs_2_ = bf16[96,4608]{1,0:T(8,128)(2,1)S(1)} collective-permute-done((bf16[96,4608]{1,0:T(8,128)(2,1)S(1)}, bf16[96,4608]{1,0:T(8,128)(2,1)S(1)}, u32[]{:S(2)}, u32[]{:S(2)}) %collective-permute-start.11) | collective-permute-done | bytes 884768 | tf_op jit(solution)/shard_map/ppermute | solution.py:232
  104.1 8.0 %products.7 = s32[96,2688]{1,0:T(8,128)S(1)} custom-call(s32[360]{0:T(512)S(1)} %reshape.8.index_ref, bf16[96,4608]{1,0:T(8,128)(2,1)S(1)} %collective-permute-done.10.refs_0_, bf16[96,5120]{1,0:T(8,128)(2,1)S(1)} %collective-permute-done.2.refs_1_, bf16[96,4608]{1,0:T(8,128)(2,1)S(1)} %collective-permute-done.11.refs_2_, bf16[40,9,128,128]{3,2,1,0:T(8,128)(2,1)} %refs_3_.9), custom_call_target="tpu_custom_call" | custom-call | flops 1 | bytes 1 | tf_op jit(solution)/shard_map/products/pallas_call | solution.py:136
  113.3 10.0 %products.8.own_ref = f32[96,5120]{1,0:T(8,128)S(1)} custom-call(s32[360]{0:T(512)S(1)} %reshape.8.index_ref, bf16[96,4608]{1,0:T(8,128)(2,1)} %collective-permute-done.refs_0_, bf16[256,5120]{1,0:T(8,128)(2,1)S(1)} %copy-done, bf16[96,4608]{1,0:T(8,128)(2,1)} %collective-permute-done.1.refs_2_, bf16[40,9,128,128]{3,2,1,0:T(8,128)(2,1)} %refs_3_.9), custom_call_target="tpu_custom_call" | custom-call | flops 1 | bytes 1 | tf_op jit(solution)/shard_map/products/pallas_call | solution.py:136
  123.4 1.6 %finish.4.refs_2_ = bf16[256,5120]{1,0:T(8,128)(2,1)} custom-call(f32[96,5120]{1,0:T(8,128)S(1)} %products.8.own_ref, s32[80,2688]{1,0:T(8,128)S(1)} %collective-permute-done.9.refs_0_.refs_1_, s32[80,2688]{1,0:T(8,128)S(1)} %collective-permute-done.9.refs_0_.refs_1_), custom_call_target="tpu_custom_call" | custom-call | flops 1 | bytes 1 | tf_op jit(solution)/shard_map/finish/pallas_call | solution.py:190
  126.0 7.7 %products.9.own_ref = f32[160,5120]{1,0:T(8,128)S(1)} custom-call(s32[360]{0:T(512)S(1)} %reshape.8.index_ref, bf16[160,4608]{1,0:T(8,128)(2,1)S(1)} %collective-permute-done.13.refs_0_, bf16[256,5120]{1,0:T(8,128)(2,1)S(1)} %copy-done, bf16[160,4608]{1,0:T(8,128)(2,1)S(1)} %collective-permute-done.14.refs_2_, bf16[40,9,128,128]{3,2,1,0:T(8,128)(2,1)} %refs_3_.9), custom_call_target="tpu_custom_call" | custom-call | flops 1 | bytes 1 | tf_op jit(solution)/shard_map/products/pallas_call | solution.py:136
  135.1 1.7 %finish.7 = bf16[256,5120]{1,0:T(8,128)(2,1)} custom-call(f32[160,5120]{1,0:T(8,128)S(1)} %products.9.own_ref, s32[96,2688]{1,0:T(8,128)S(1)} %collective-permute-done.15.refs_0_.refs_1_, s32[96,2688]{1,0:T(8,128)S(1)} %collective-permute-done.15.refs_0_.refs_1_, bf16[256,5120]{1,0:T(8,128)(2,1)} %finish.6.refs_2_), custom_call_target="tpu_custom_call", output_to_operand_aliasing={{}: (3, {})} | custom-call | flops 1 | bytes 1 | tf_op jit(solution)/shard_map/finish/pallas_call | solution.py:190
  (35 shorter events, 10.4 us)
Async XLA Ops:
  0.0 12.1 %copy-start = (bf16[256,5120]{1,0:T(8,128)(2,1)S(1)}, bf16[256,5120]{1,0:T(8,128)(2,1)}, u32[]{:S(2)}) copy-start(bf16[256,5120]{1,0:T(8,128)(2,1)} %refs_1_.3) | copy-start | bytes 7864324
  2.2 11.1 %copy-start.1 = (s32[40,9]{0,1:T(8,128)S(1)}, s32[40,9]{0,1:T(8,128)}, u32[]{:S(2)}) copy-start(s32[40,9]{0,1:T(8,128)} %param.6) | copy-start | bytes 4324
  2.2 11.1 %copy-start.2 = (s32[40]{0:T(128)S(1)}, s32[40]{0:T(128)}, u32[]{:S(2)}) copy-start(s32[40]{0:T(128)} %param.7) | copy-start | bytes 484
  2.2 19.4 %collective-permute-start.6 = (bf16[80,5120]{1,0:T(8,128)(2,1)}, bf16[80,5120]{1,0:T(8,128)(2,1)}, u32[]{:S(2)}, u32[]{:S(2)}) collective-permute-start(bf16[80,5120]{1,0:T(8,128)(2,1)} %slice.55), channel_id=1, source_target_pairs={{0,1},{1,0},{2,3},{3,2},{4,5},{5,4},{6,7},{7,6},{8,9},{9,8},{10,11... | collective-permute-start | bytes 2457608 | tf_op jit(solution)/shard_map/ppermute | solution.py:235
  6.2 24.7 %collective-permute-start.1 = (bf16[96,4608]{1,0:T(8,128)(2,1)}, bf16[96,4608]{1,0:T(8,128)(2,1)}, u32[]{:S(2)}, u32[]{:S(2)}) collective-permute-start(bf16[96,4608]{1,0:T(8,128)(2,1)} %get-tuple-element.27), channel_id=1, source_target_pairs={{2,0},{4,2},{6,4},{8,6},{10,8},{12,10},{14,12},{16,14},{18,16},{20... | collective-permute-start | bytes 2654216 | tf_op jit(solution)/shard_map/ppermute | solution.py:232
  9.1 29.4 %collective-permute-start = (bf16[96,4608]{1,0:T(8,128)(2,1)}, bf16[96,4608]{1,0:T(8,128)(2,1)}, u32[]{:S(2)}, u32[]{:S(2)}) collective-permute-start(bf16[96,4608]{1,0:T(8,128)(2,1)} %get-tuple-element.28), channel_id=1, source_target_pairs={{0,2},{2,4},{4,6},{6,8},{8,10},{10,12},{12,14},{14,16},{16,18},{18... | collective-permute-start | bytes 2654216 | tf_op jit(solution)/shard_map/ppermute | solution.py:232
  13.1 26.0 %collective-permute-start.3 = (bf16[80,5120]{1,0:T(8,128)(2,1)}, bf16[80,5120]{1,0:T(8,128)(2,1)S(1)}, u32[]{:S(2)}, u32[]{:S(2)}) collective-permute-start(bf16[80,5120]{1,0:T(8,128)(2,1)} %slice.52), channel_id=1, source_target_pairs={{0,1},{1,0},{2,3},{3,2},{4,5},{5,4},{6,7},{7,6},{8,9},{9,8},{10,11... | collective-permute-start | bytes 2457608 | tf_op jit(solution)/shard_map/ppermute | solution.py:235
  23.1 23.7 %collective-permute-start.8 = (bf16[80,4608]{1,0:T(8,128)(2,1)S(1)}, bf16[80,4608]{1,0:T(8,128)(2,1)S(1)}, u32[]{:S(2)}, u32[]{:S(2)}) collective-permute-start(bf16[80,4608]{1,0:T(8,128)(2,1)S(1)} %get-tuple-element.33), channel_id=1, source_target_pairs={{2,0},{4,2},{6,4},{8,6},{10,8},{12,10},{14,12},{16,14},{18,16},{20... | collective-permute-start | bytes 2211848 | tf_op jit(solution)/shard_map/ppermute | solution.py:232
  27.8 26.4 %collective-permute-start.7 = (bf16[80,4608]{1,0:T(8,128)(2,1)S(1)}, bf16[80,4608]{1,0:T(8,128)(2,1)S(1)}, u32[]{:S(2)}, u32[]{:S(2)}) collective-permute-start(bf16[80,4608]{1,0:T(8,128)(2,1)S(1)} %get-tuple-element.34), channel_id=1, source_target_pairs={{0,2},{2,4},{4,6},{6,8},{8,10},{10,12},{12,14},{14,16},{16,18},{18... | collective-permute-start | bytes 2211848 | tf_op jit(solution)/shard_map/ppermute | solution.py:232
  38.6 24.4 %collective-permute-start.2 = (bf16[96,5120]{1,0:T(8,128)(2,1)S(1)}, bf16[96,5120]{1,0:T(8,128)(2,1)S(1)}, u32[]{:S(2)}, u32[]{:S(2)}) collective-permute-start(bf16[96,5120]{1,0:T(8,128)(2,1)S(1)} %slice.49), channel_id=1, source_target_pairs={{0,1},{1,0},{2,3},{3,2},{4,5},{5,4},{6,7},{7,6},{8,9},{9,8},{10,11... | collective-permute-start | bytes 2949128 | tf_op jit(solution)/shard_map/ppermute | solution.py:235
  39.2 30.6 %collective-permute-start.5 = (bf16[80,4608]{1,0:T(8,128)(2,1)S(1)}, bf16[80,4608]{1,0:T(8,128)(2,1)S(1)}, u32[]{:S(2)}, u32[]{:S(2)}) collective-permute-start(bf16[80,4608]{1,0:T(8,128)(2,1)S(1)} %get-tuple-element.35), channel_id=1, source_target_pairs={{2,0},{4,2},{6,4},{8,6},{10,8},{12,10},{14,12},{16,14},{18,16},{20... | collective-permute-start | bytes 2211848 | tf_op jit(solution)/shard_map/ppermute | solution.py:232
  42.7 27.1 %collective-permute-start.4 = (bf16[80,4608]{1,0:T(8,128)(2,1)S(1)}, bf16[80,4608]{1,0:T(8,128)(2,1)S(1)}, u32[]{:S(2)}, u32[]{:S(2)}) collective-permute-start(bf16[80,4608]{1,0:T(8,128)(2,1)S(1)} %get-tuple-element.36), channel_id=1, source_target_pairs={{0,2},{2,4},{4,6},{6,8},{8,10},{10,12},{12,14},{14,16},{16,18},{18... | collective-permute-start | bytes 2211848 | tf_op jit(solution)/shard_map/ppermute | solution.py:232
  62.7 17.2 %collective-permute-start.9 = (s32[80,2688]{1,0:T(8,128)S(1)}, s32[80,2688]{1,0:T(8,128)S(1)}, u32[]{:S(2)}, u32[]{:S(2)}) collective-permute-start(s32[80,2688]{1,0:T(8,128)S(1)} %products.6), channel_id=1, source_target_pairs={{0,1},{1,0},{2,3},{3,2},{4,5},{5,4},{6,7},{7,6},{8,9},{9,8},{10,11... | collective-permute-start | bytes 2580488 | tf_op jit(solution)/shard_map/ppermute | solution.py:235
  63.1 41.0 %collective-permute-start.11 = (bf16[96,4608]{1,0:T(8,128)(2,1)S(1)}, bf16[96,4608]{1,0:T(8,128)(2,1)S(1)}, u32[]{:S(2)}, u32[]{:S(2)}) collective-permute-start(bf16[96,4608]{1,0:T(8,128)(2,1)S(1)} %get-tuple-element.31), channel_id=1, source_target_pairs={{2,0},{4,2},{6,4},{8,6},{10,8},{12,10},{14,12},{16,14},{18,16},{20... | collective-permute-start | bytes 2654216 | tf_op jit(solution)/shard_map/ppermute | solution.py:232
  65.0 39.1 %collective-permute-start.10 = (bf16[96,4608]{1,0:T(8,128)(2,1)S(1)}, bf16[96,4608]{1,0:T(8,128)(2,1)S(1)}, u32[]{:S(2)}, u32[]{:S(2)}) collective-permute-start(bf16[96,4608]{1,0:T(8,128)(2,1)S(1)} %get-tuple-element.32), channel_id=1, source_target_pairs={{0,2},{2,4},{4,6},{6,8},{8,10},{10,12},{12,14},{14,16},{16,18},{18... | collective-permute-start | bytes 2654216 | tf_op jit(solution)/shard_map/ppermute | solution.py:232
  79.9 32.3 %collective-permute-start.12 = (s32[80,2688]{1,0:T(8,128)S(1)}, s32[80,2688]{1,0:T(8,128)S(1)}, u32[]{:S(2)}, u32[]{:S(2)}) collective-permute-start(s32[80,2688]{1,0:T(8,128)S(1)} %products.5), channel_id=1, source_target_pairs={{0,1},{1,0},{2,3},{3,2},{4,5},{5,4},{6,7},{7,6},{8,9},{9,8},{10,11... | collective-permute-start | bytes 2580488 | tf_op jit(solution)/shard_map/ppermute | solution.py:235
  81.2 44.8 %collective-permute-start.13 = (bf16[160,4608]{1,0:T(8,128)(2,1)S(1)}, bf16[160,4608]{1,0:T(8,128)(2,1)S(1)}, u32[]{:S(2)}, u32[]{:S(2)}) collective-permute-start(bf16[160,4608]{1,0:T(8,128)(2,1)S(1)} %get-tuple-element.20), channel_id=1, source_target_pairs={{0,2},{2,4},{4,6},{6,8},{8,10},{10,12},{12,14},{14,16},{16,18},{18... | collective-permute-start | bytes 4423688 | tf_op jit(solution)/shard_map/ppermute | solution.py:232
  84.9 41.1 %collective-permute-start.14 = (bf16[160,4608]{1,0:T(8,128)(2,1)S(1)}, bf16[160,4608]{1,0:T(8,128)(2,1)S(1)}, u32[]{:S(2)}, u32[]{:S(2)}) collective-permute-start(bf16[160,4608]{1,0:T(8,128)(2,1)S(1)} %get-tuple-element.21), channel_id=1, source_target_pairs={{2,0},{4,2},{6,4},{8,6},{10,8},{12,10},{14,12},{16,14},{18,16},{20... | collective-permute-start | bytes 4423688 | tf_op jit(solution)/shard_map/ppermute | solution.py:232
  112.2 23.0 %collective-permute-start.15 = (s32[96,2688]{1,0:T(8,128)S(1)}, s32[96,2688]{1,0:T(8,128)S(1)}, u32[]{:S(2)}, u32[]{:S(2)}) collective-permute-start(s32[96,2688]{1,0:T(8,128)S(1)} %products.7), channel_id=1, source_target_pairs={{0,1},{1,0},{2,3},{3,2},{4,5},{5,4},{6,7},{7,6},{8,9},{9,8},{10,11... | collective-permute-start | bytes 3096584 | tf_op jit(solution)/shard_map/ppermute | solution.py:235
where the time goes:
time: 137 us
  Pallas kernels  48.2 us (35%)
  waiting for transfers between devices  42.6 us (31%)
  starting transfers between devices  37.6 us (27%)
  local copies, waits for them, and re-layouts  8.11 us (6%)
    pallas_call x5, Pallas kernels, products(): pl.pallas_call(functools.partial(products_kernel, plan, group, slots, blo...  42.5 us
    ppermute x5, starting transfers between devices, halo(): lax.ppermute(edges[0], 'basis', up)  18.7 us
    ppermute x5, waiting for transfers between devices, halo(): lax.ppermute(edges[1], 'basis', down)  17.4 us
    ppermute x5, waiting for transfers between devices, halo(): lax.ppermute(edges[0], 'basis', up)  14.9 us
    ppermute x5, starting transfers between devices, halo(): lax.ppermute(edges[1], 'basis', down)  14.8 us
    ppermute x6, waiting for transfers between devices, shifted(): lax.ppermute(piece, 'state', [(i, (i + shift) % state_size) for i in rang...  10.2 us
    pallas_call x4, Pallas kernels, finish(): pl.pallas_call(functools.partial(finish_kernel, len(coded), block, pairs)...  5.76 us
    slice x5, local copies, waits for them, and re-layouts, edges_of(): edges = (piece[:, width - reach:], piece[:, :reach])  4.64 us
  transfers between devices with their start and end apart: 16, of which 7 were waited for; matrix products, arithmetic and copies ran while one was open for 4% of the time, Pallas kernels for 34%

commit v1 on v0

v1 whole, which is shorter than its diff:
```python
import functools
import math

import jax
import jax.numpy as jnp
from jax import lax
from jax.experimental import pallas as pl
from jax.experimental.pallas import tpu as pltpu
from jax.sharding import PartitionSpec as P

W = 36
VMEM_LIMIT = 32 * 1024 * 1024
TOP = 32767.0
FINE = 65536.0
SMALLEST = 2.0**-100


def after(array, *others):
    return lax.optimization_barrier((array, *others))[0]


def fill(sources, starts, ext, sems):
    copies, column = [], 0
    for n, (source, start) in enumerate(zip(sources, starts)):
        width = source.shape[1]
        target = ext.at[:, pl.ds(column, width)]
        copies.append(pltpu.make_async_copy(source.at[pl.ds(start, ext.shape[0])], target, sems.at[n]))
        copies[-1].start()
        column += width
    return copies


def row_sums(index_ref, row, slots, block, ext, panel_ref):
    picked = jnp.concatenate(
        [
            ext[:, pl.ds(pl.multiple_of(index_ref[row * slots + slot] * block, block), block)]
            for slot in range(slots)
        ],
        axis=1,
    )
    panel = jnp.concatenate([panel_ref[slot] for slot in range(slots)], axis=1)
    return lax.dot_general(
        picked, panel, (((1,), (1,)), ((), ())), preferred_element_type=jnp.float32
    )


def level_code(top):
    return jnp.ceil(jnp.log2(jnp.maximum(top, SMALLEST)) * FINE).astype(jnp.int32)


def level_of(code):
    return jnp.exp2(code.astype(jnp.float32) * (1.0 / FINE))


def code_into(out_ref, first, block, words, sums):
    lane = lax.broadcasted_iota(jnp.int32, (out_ref.shape[0], block), 1)
    codes = out_ref[:, words * block :]
    values = []
    for member, mine in enumerate(sums):
        code = level_code(jnp.max(jnp.abs(mine), axis=1, keepdims=True))
        codes = jnp.where(lane == first + member, code, codes)
        scaled = jnp.round(mine * (TOP / level_of(code)))
        values.append(jnp.clip(scaled, -TOP, TOP).astype(jnp.int32))
    out_ref[:, words * block :] = codes
    for pair in range(len(sums) // 2):
        word = (values[2 * pair + 1] << 16) | (values[2 * pair] & 0xFFFF)
        at = pl.multiple_of((first // 2 + pair) * block, block)
        out_ref[:, pl.ds(at, block)] = word


def start_panels(blocks_ref, panels, sems):
    piece = panels.shape[0] // sems.shape[0]

    def copy(n):
        here = pl.ds(n * piece, piece)
        return pltpu.make_async_copy(blocks_ref.at[here], panels.at[here], sems.at[n])

    def wait(step, group):
        for n in range(group // piece):
            copy(step * (group // piece) + n).wait()

    for n in range(sems.shape[0]):
        copy(n).start()
    return wait


def coded_kernel(group, slots, block, words, index_ref, *refs):
    sources, (blocks_ref, out_ref, ext, panels, sems, panel_sems) = refs[:3], refs[3:]
    size = ext.shape[0]
    copies = fill(sources, (0, 0, 0), ext, sems)
    wait = start_panels(blocks_ref, panels, panel_sems)
    ext[:, ext.shape[1] - block :] = jnp.zeros((size, block), ext.dtype)
    out_ref[:, words * block :] = jnp.zeros((size, block), jnp.int32)
    for copy in copies:
        copy.wait()

    @pl.loop(0, panels.shape[0] // group)
    def _(step):
        wait(step, group)
        first = step * group
        sums = [
            row_sums(index_ref, first + member, slots, block, ext, panels.at[first + member])
            for member in range(group)
        ]
        code_into(out_ref, first, block, words, sums)


def group_of(rows):
    return 8 if rows % 8 == 0 else 2


def coded_products(index, left, own, right, blocks):
    rows, slots, block, _ = blocks.shape
    size, words, group = own.shape[0], rows // 2, group_of(rows)
    width = 2 * left.shape[1] + own.shape[1] + block
    anywhere = pl.BlockSpec(memory_space=pl.ANY)
    return pl.pallas_call(
        functools.partial(coded_kernel, group, slots, block, words),
        out_shape=jax.ShapeDtypeStruct((size, (words + 1) * block), jnp.int32),
        in_specs=[pl.BlockSpec(memory_space=pltpu.SMEM)] + [anywhere] * 3 + [pl.BlockSpec(memory_space=pltpu.HBM)],
        out_specs=pl.BlockSpec(memory_space=pltpu.VMEM),
        scratch_shapes=[
            pltpu.VMEM((size, width), own.dtype),
            pltpu.VMEM(blocks.shape, blocks.dtype),
            pltpu.SemaphoreType.DMA((3,)),
            pltpu.SemaphoreType.DMA((rows // 2,)),
        ],
        compiler_params=pltpu.CompilerParams(vmem_limit_bytes=VMEM_LIMIT),
        cost_estimate=pl.CostEstimate(flops=1, bytes_accessed=1, transcendentals=0),
        name="coded_products",
    )(index, left, own, right, pltpu.with_memory_space_constraint(blocks, pltpu.HBM))


def decoded(coded_ref, row, half, at, block, words):
    lane = lax.broadcasted_iota(jnp.int32, (coded_ref.shape[0], block), 1)
    codes = coded_ref[:, words * block :].astype(jnp.float32)
    code = jnp.sum(jnp.where(lane == row, codes, 0.0), axis=1, keepdims=True)
    word = coded_ref[:, pl.ds(at, block)]
    value = (word >> 16) if half else ((word << 16) >> 16)
    return value.astype(jnp.float32) * (jnp.exp2(code * (1.0 / FINE)) * (1.0 / TOP))


def final_kernel(group, slots, block, words, starts, pieces, aliased, index_ref, *refs):
    count = sum(partials for _, _, _, partials in pieces)
    sources, blocks_ref, coded = refs[:3], refs[3], refs[4 : 4 + count]
    refs = refs[4 + count + aliased :]
    out_ref, ext, panels, result, sems, panel_sems, coded_sems, out_sems = refs[:8]
    held = refs[8:]
    size, rows = ext.shape[0], panels.shape[0]
    copies = fill(sources, starts, ext, sems)
    n = 0
    for _, length, start, partials in pieces:
        for _ in range(partials):
            source = coded[n].at[pl.ds(start, length)]
            copies.append(pltpu.make_async_copy(source, held[n], coded_sems.at[n]))
            copies[-1].start()
            n += 1
    wait = start_panels(blocks_ref, panels, panel_sems)
    ext[:, ext.shape[1] - block :] = jnp.zeros((size, block), ext.dtype)
    for copy in copies:
        copy.wait()

    def result_copy(step):
        columns = pl.ds(pl.multiple_of(step * group * block, block), group * block)
        target = out_ref.at[pl.ds(starts[1], size), columns]
        return pltpu.make_async_copy(result.at[:, columns], target, out_sems.at[step])

    @pl.loop(0, rows // group)
    def _(step):
        wait(step, group)
        first = step * group
        sums = [
            row_sums(index_ref, first + member, slots, block, ext, panels.at[first + member])
            for member in range(group)
        ]
        for member, mine in enumerate(sums):
            at = pl.multiple_of((first // 2 + member // 2) * block, block)
            column = pl.multiple_of((first + member) * block, block)
            n = 0
            for offset, length, _, partials in pieces:
                total = mine[offset : offset + length]
                for _ in range(partials):
                    total = total + decoded(held[n], first + member, member % 2, at, block, words)
                    n += 1
                result[offset : offset + length, pl.ds(column, block)] = total.astype(result.dtype)
        result_copy(step).start()

    @pl.loop(0, rows // group)
    def _(step):
        result_copy(step).wait()


def final_products(index, left, own, right, starts, size, blocks, pieces, out):
    rows, slots, block, _ = blocks.shape
    words, group = rows // 2, group_of(rows)
    width = own.shape[1]
    arrays = [array for _, _, _, some in pieces for array in some]
    operands = [index, left, own, right, pltpu.with_memory_space_constraint(blocks, pltpu.HBM), *arrays]
    anywhere = pl.BlockSpec(memory_space=pl.ANY)
    aliases = {}
    if out is not None:
        aliases = {len(operands): 0}
        operands.append(out)
    in_specs = [pl.BlockSpec(memory_space=pltpu.SMEM)] + [anywhere] * (len(operands) - 1)
    in_specs[4] = pl.BlockSpec(memory_space=pltpu.HBM)
    shapes = tuple((offset, length, start, len(some)) for offset, length, start, some in pieces)
    return pl.pallas_call(
        functools.partial(final_kernel, group, slots, block, words, starts, shapes, len(aliases)),
        out_shape=jax.ShapeDtypeStruct(own.shape, own.dtype),
        in_specs=in_specs,
        out_specs=anywhere,
        scratch_shapes=[
            pltpu.VMEM((size, 2 * left.shape[1] + width + block), own.dtype),
            pltpu.VMEM(blocks.shape, blocks.dtype),
            pltpu.VMEM((size, width), own.dtype),
            pltpu.SemaphoreType.DMA((3,)),
            pltpu.SemaphoreType.DMA((rows // 2,)),
            pltpu.SemaphoreType.DMA((len(arrays),)),
            pltpu.SemaphoreType.DMA((rows // group,)),
        ]
        + [
            pltpu.VMEM((length, (words + 1) * block), jnp.int32)
            for _, length, _, partials in shapes
            for _ in range(partials)
        ],
        input_output_aliases=aliases,
        compiler_params=pltpu.CompilerParams(vmem_limit_bytes=VMEM_LIMIT),
        cost_estimate=pl.CostEstimate(flops=1, bytes_accessed=1, transcendentals=0),
        name="final_products",
    )(*operands)


def starts_of(sizes):
    return [sum(sizes[:i]) for i in range(len(sizes))]


def on_device(vectors, blocks, columns, counts):
    states, width = vectors.shape
    rows, slots, block, _ = blocks.shape
    reach = W * block
    basis_size, state_size = lax.axis_size("basis"), lax.axis_size("state")
    if states % 256 == 0:
        sizes = (5 * states // 16, 5 * states // 16, 3 * states // 8)
        own_sizes = (3 * states // 8, 5 * states // 8)
    else:
        sizes, own_sizes = (states,), (states,)
    starts, own_starts = starts_of(sizes), starts_of(own_sizes)

    slot_index = lax.axis_index("state") * slots + jnp.arange(slots, dtype=jnp.int32)
    relative = columns - (lax.axis_index("basis") * rows - W)
    zeros_at = rows + 2 * W
    index = jnp.where(slot_index[None, :] < counts[:, None], relative, zeros_at).reshape(-1)

    up = [(i, i + 1) for i in range(basis_size - 1)]
    down = [(i + 1, i) for i in range(basis_size - 1)]

    def edges_of(piece, *others):
        edges = (piece[:, width - reach :], piece[:, :reach])
        return lax.optimization_barrier((*edges, *others))[:2] if others else edges

    def halo(edges):
        return lax.ppermute(edges[0], "basis", up), lax.ppermute(edges[1], "basis", down)

    def shifted(piece, shift):
        return lax.ppermute(piece, "state", [(i, (i + shift) % state_size) for i in range(state_size)])

    def own_edges(part, *others):
        return edges_of(vectors[own_starts[part] : own_starts[part] + own_sizes[part]], *others)

    messages = [(shift, c) for shift in range(1, state_size) for c in range(len(sizes))]
    count = len(messages)
    theirs, edges, ends, sent, received = [], [], [], [], []
    first_edges = own_edges(0)
    first = halo(first_edges)
    for n, (shift, c) in enumerate(messages):
        source = after(vectors, *(first_edges if n == 1 else first)) if n else vectors
        theirs.append(shifted(source[starts[c] : starts[c] + sizes[c]], shift))

    def compute(n):
        later = edges[n + 1] if n + 1 < len(edges) else ()
        ready = after(index, *later) if later else index
        sent.append(coded_products(ready, ends[n][0], theirs[n], ends[n][1], blocks))
        message = after(sent[n], received[n - 1]) if n else sent[n]
        received.append(shifted(message, -messages[n][0]))

    for n in range(count):
        edges.append(edges_of(theirs[n]))
        ends.append(halo(edges[n]))
        if n:
            compute(n - 1)
    own_ends = [first]
    if len(own_sizes) > 1:
        edges.append(own_edges(1, *ends[-1], *sent[-1:], *received[:1]))
        own_ends.append(halo(edges[-1]))
    compute(count - 1)

    out = None
    for part, own_size in enumerate(own_sizes):
        own_start, pieces = own_starts[part], []
        for c, size in enumerate(sizes):
            at = max(own_start, starts[c])
            end = min(own_start + own_size, starts[c] + size)
            if at < end:
                arrays = [received[n] for n in range(count) if messages[n][1] == c]
                pieces.append((at - own_start, end - at, at - starts[c], arrays))
        left, right = own_ends[part]
        ready = after(index, sent[-1], out) if part else after(index, sent[-1])
        out = final_products(
            ready, left, vectors, right, (0, own_start, 0), own_size, blocks, pieces, out
        )
    return out


def solution(mesh):
    in_specs = (
        P("state", "basis"),
        P("basis", "state", None, None),
        P("basis", "state"),
        P("basis"),
    )
    out_specs = P("state", "basis")
    return jax.shard_map(
        on_device, mesh=mesh, in_specs=in_specs, out_specs=out_specs, check_vma=False
    )
```

time: 137 us -> 150 us (1.095)
  waiting for transfers between devices: 42.6 us -> 62.6 us
  Pallas kernels: 48.2 us -> 42.6 us
    ppermute x5, waiting for transfers between devices: 14.9 us -> 26.8 us  [halo(): lax.ppermute(edges[0], 'basis', up)]
    pallas_call x9 -> x5, Pallas kernels: 48.2 us -> 42.6 us  [the longest x3 24.8 us: coded_products(): pl.pallas_call(functools.partial(coded_kernel, group, slots, block, words...]
    ppermute x5, waiting for transfers between devices: 17.4 us -> 22.8 us  [halo(): lax.ppermute(edges[1], 'basis', down)]
    ppermute x6, waiting for transfers between devices: 10.2 us -> 13 us  [shifted(): lax.ppermute(piece, 'state', [(i, (i + shift) % state_size) for i in rang...]
    ppermute x5, starting transfers between devices: 18.7 us -> 16.9 us  [halo(): lax.ppermute(edges[0], 'basis', up)]
  transfers between devices with their start and end apart: 16 -> 16, of which waited for: 7 -> 9; matrix products, arithmetic and copies ran while one was open for 4% -> 4% of each run, Pallas kernels for 34% -> 22%
where the time goes in v1:
time: 150 us
  waiting for transfers between devices  62.6 us (42%)
  Pallas kernels  42.6 us (28%)
  starting transfers between devices  36.3 us (24%)
  local copies, waits for them, and re-layouts  8.12 us (5%)
    ppermute x5, waiting for transfers between devices, halo(): lax.ppermute(edges[0], 'basis', up)  26.8 us
    pallas_call x3, Pallas kernels, coded_products(): pl.pallas_call(functools.partial(coded_kernel, group, slots, block, words...  24.8 us
    ppermute x5, waiting for transfers between devices, halo(): lax.ppermute(edges[1], 'basis', down)  22.8 us
    pallas_call x2, Pallas kernels, final_products(): pl.pallas_call(functools.partial(final_kernel, group, slots, block, words...  17.8 us
    ppermute x5, starting transfers between devices, halo(): lax.ppermute(edges[0], 'basis', up)  16.9 us
    ppermute x5, starting transfers between devices, halo(): lax.ppermute(edges[1], 'basis', down)  15.2 us
    ppermute x6, waiting for transfers between devices, shifted(): lax.ppermute(piece, 'state', [(i, (i + shift) % state_size) for i in rang...  13 us
    slice x5, local copies, waits for them, and re-layouts, edges_of(): edges = (piece[:, width - reach:], piece[:, :reach])  4.65 us
  transfers between devices with their start and end apart: 16, of which 9 were waited for; matrix products, arithmetic and copies ran while one was open for 4% of the time, Pallas kernels for 22%

profile of v1, /device:TPU:9, one launch (start us, length us, event | category | flops | bytes accessed | tf_op | source)
XLA Modules:
  0.0 149.9 jit_solution(3315015612474162332)
XLA Ops:
  0.0 2.2 %slice.55 = bf16[80,5120]{1,0:T(8,128)(2,1)} slice(bf16[256,5120]{1,0:T(8,128)(2,1)} %refs_1_.3), slice={[0:80], [0:5120]} | slice | bytes 1638400 | tf_op jit(solution)/shard_map/slice | solution.py:277
  3.4 2.8 %fusion = (bf16[96,4608]{1,0:T(8,128)(2,1)}, bf16[96,4608]{1,0:T(8,128)(2,1)}) fusion(bf16[256,5120]{1,0:T(8,128)(2,1)} %refs_1_.3), kind=kLoop, calls=%fused_computation.2 | loop fusion | bytes 3538944 | tf_op jit(solution)/shard_map/slice | solution.py:258
  6.2 2.9 %collective-permute-start.1 = (bf16[96,4608]{1,0:T(8,128)(2,1)}, bf16[96,4608]{1,0:T(8,128)(2,1)}, u32[]{:S(2)}, u32[]{:S(2)}) collective-permute-start(bf16[96,4608]{1,0:T(8,128)(2,1)} %get-tuple-element.27), channel_id=1, source_target_pairs={{2,0},{4,2},{6,4},{8,6},{10,8},{12,10},{14,12},{16,14},{18,16},{20... | collective-permute-start | bytes 2654216 | tf_op jit(solution)/shard_map/ppermute | solution.py:262
  9.1 3.0 %collective-permute-start = (bf16[96,4608]{1,0:T(8,128)(2,1)}, bf16[96,4608]{1,0:T(8,128)(2,1)}, u32[]{:S(2)}, u32[]{:S(2)}) collective-permute-start(bf16[96,4608]{1,0:T(8,128)(2,1)} %get-tuple-element.28), channel_id=1, source_target_pairs={{0,2},{2,4},{4,6},{6,8},{8,10},{10,12},{12,14},{14,16},{16,18},{18... | collective-permute-start | bytes 2654216 | tf_op jit(solution)/shard_map/ppermute | solution.py:262
  13.7 8.0 %collective-permute-done.8.refs_1_ = bf16[80,5120]{1,0:T(8,128)(2,1)} collective-permute-done((bf16[80,5120]{1,0:T(8,128)(2,1)}, bf16[80,5120]{1,0:T(8,128)(2,1)}, u32[]{:S(2)}, u32[]{:S(2)}) %collective-permute-start.8) | collective-permute-done | bytes 819232 | tf_op jit(solution)/shard_map/ppermute | solution.py:265
  23.1 4.6 %collective-permute-start.10 = (bf16[80,4608]{1,0:T(8,128)(2,1)S(1)}, bf16[80,4608]{1,0:T(8,128)(2,1)S(1)}, u32[]{:S(2)}, u32[]{:S(2)}) collective-permute-start(bf16[80,4608]{1,0:T(8,128)(2,1)S(1)} %get-tuple-element.33), channel_id=1, source_target_pairs={{2,0},{4,2},{6,4},{8,6},{10,8},{12,10},{14,12},{16,14},{18,16},{20... | collective-permute-start | bytes 2211848 | tf_op jit(solution)/shard_map/ppermute | solution.py:262
  27.8 3.0 %collective-permute-start.9 = (bf16[80,4608]{1,0:T(8,128)(2,1)S(1)}, bf16[80,4608]{1,0:T(8,128)(2,1)S(1)}, u32[]{:S(2)}, u32[]{:S(2)}) collective-permute-start(bf16[80,4608]{1,0:T(8,128)(2,1)S(1)} %get-tuple-element.34), channel_id=1, source_target_pairs={{0,2},{2,4},{4,6},{6,8},{8,10},{10,12},{12,14},{14,16},{16,18},{18... | collective-permute-start | bytes 2211848 | tf_op jit(solution)/shard_map/ppermute | solution.py:262
  30.9 7.6 %collective-permute-done.refs_0_ = bf16[96,4608]{1,0:T(8,128)(2,1)} collective-permute-done((bf16[96,4608]{1,0:T(8,128)(2,1)}, bf16[96,4608]{1,0:T(8,128)(2,1)}, u32[]{:S(2)}, u32[]{:S(2)}) %collective-permute-start) | collective-permute-done | bytes 884768 | tf_op jit(solution)/shard_map/ppermute | solution.py:262
  39.2 3.5 %collective-permute-start.7 = (bf16[80,4608]{1,0:T(8,128)(2,1)S(1)}, bf16[80,4608]{1,0:T(8,128)(2,1)S(1)}, u32[]{:S(2)}, u32[]{:S(2)}) collective-permute-start(bf16[80,4608]{1,0:T(8,128)(2,1)S(1)} %get-tuple-element.35), channel_id=1, source_target_pairs={{2,0},{4,2},{6,4},{8,6},{10,8},{12,10},{14,12},{16,14},{18,16},{20... | collective-permute-start | bytes 2211848 | tf_op jit(solution)/shard_map/ppermute | solution.py:262
  42.7 4.2 %collective-permute-start.6 = (bf16[80,4608]{1,0:T(8,128)(2,1)S(1)}, bf16[80,4608]{1,0:T(8,128)(2,1)S(1)}, u32[]{:S(2)}, u32[]{:S(2)}) collective-permute-start(bf16[80,4608]{1,0:T(8,128)(2,1)S(1)} %get-tuple-element.36), channel_id=1, source_target_pairs={{0,2},{2,4},{4,6},{6,8},{8,10},{10,12},{12,14},{14,16},{16,18},{18... | collective-permute-start | bytes 2211848 | tf_op jit(solution)/shard_map/ppermute | solution.py:262
  46.9 7.3 %collective-permute-done.9.refs_0_ = bf16[80,4608]{1,0:T(8,128)(2,1)S(1)} collective-permute-done((bf16[80,4608]{1,0:T(8,128)(2,1)S(1)}, bf16[80,4608]{1,0:T(8,128)(2,1)S(1)}, u32[]{:S(2)}, u32[]{:S(2)}) %collective-permute-start.9) | collective-permute-done | bytes 737312 | tf_op jit(solution)/shard_map/ppermute | solution.py:262
  54.2 8.5 %coded_products.4 = s32[80,2688]{1,0:T(8,128)S(1)} custom-call(s32[360]{0:T(512)S(1)} %reshape.8.index_ref, bf16[80,4608]{1,0:T(8,128)(2,1)S(1)} %collective-permute-done.9.refs_0_, bf16[80,5120]{1,0:T(8,128)(2,1)} %collective-permute-done.8.refs_1_, bf16[80,4608]{1,0:T(8,128)(2,1)S(1)} %collective-permute-done.10.refs_2_, bf16[40,9,128,128]{3,2,1,0:T(8,128)(2,1)} %refs_3_.9), custom_call_target="tpu_custom_call" | custom-call | flops 1 | bytes 1 | tf_op jit(solution)/shard_map/coded_products/pallas_call | solution.py:117
  63.1 1.9 %collective-permute-start.4 = (bf16[96,4608]{1,0:T(8,128)(2,1)S(1)}, bf16[96,4608]{1,0:T(8,128)(2,1)S(1)}, u32[]{:S(2)}, u32[]{:S(2)}) collective-permute-start(bf16[96,4608]{1,0:T(8,128)(2,1)S(1)} %get-tuple-element.31), channel_id=1, source_target_pairs={{2,0},{4,2},{6,4},{8,6},{10,8},{12,10},{14,12},{16,14},{18,16},{20... | collective-permute-start | bytes 2654216 | tf_op jit(solution)/shard_map/ppermute | solution.py:262
  65.0 4.7 %collective-permute-start.3 = (bf16[96,4608]{1,0:T(8,128)(2,1)S(1)}, bf16[96,4608]{1,0:T(8,128)(2,1)S(1)}, u32[]{:S(2)}, u32[]{:S(2)}) collective-permute-start(bf16[96,4608]{1,0:T(8,128)(2,1)S(1)} %get-tuple-element.32), channel_id=1, source_target_pairs={{0,2},{2,4},{4,6},{6,8},{8,10},{10,12},{12,14},{14,16},{16,18},{18... | collective-permute-start | bytes 2654216 | tf_op jit(solution)/shard_map/ppermute | solution.py:262
  69.8 8.3 %coded_products.3 = s32[80,2688]{1,0:T(8,128)S(1)} custom-call(s32[360]{0:T(512)S(1)} %reshape.8.index_ref, bf16[80,4608]{1,0:T(8,128)(2,1)S(1)} %collective-permute-done.6.refs_0_, bf16[80,5120]{1,0:T(8,128)(2,1)S(1)} %collective-permute-done.5.refs_1_, bf16[80,4608]{1,0:T(8,128)(2,1)S(1)} %collective-permute-done.7.refs_2_, bf16[40,9,128,128]{3,2,1,0:T(8,128)(2,1)} %refs_3_.9), custom_call_target="tpu_custom_call" | custom-call | flops 1 | bytes 1 | tf_op jit(solution)/shard_map/coded_products/pallas_call | solution.py:117
  78.1 1.8 %collective-permute-done.11.refs_4_ = s32[80,2688]{1,0:T(8,128)S(1)} collective-permute-done((s32[80,2688]{1,0:T(8,128)S(1)}, s32[80,2688]{1,0:T(8,128)S(1)}, u32[]{:S(2)}, u32[]{:S(2)}) %collective-permute-start.11) | collective-permute-done | bytes 860192 | tf_op jit(solution)/shard_map/ppermute | solution.py:265
  81.2 22.7 %collective-permute-done.4.refs_2_ = bf16[96,4608]{1,0:T(8,128)(2,1)S(1)} collective-permute-done((bf16[96,4608]{1,0:T(8,128)(2,1)S(1)}, bf16[96,4608]{1,0:T(8,128)(2,1)S(1)}, u32[]{:S(2)}, u32[]{:S(2)}) %collective-permute-start.4) | collective-permute-done | bytes 884768 | tf_op jit(solution)/shard_map/ppermute | solution.py:262
  103.8 1.9 %collective-permute-start.13 = (bf16[160,4608]{1,0:T(8,128)(2,1)S(1)}, bf16[160,4608]{1,0:T(8,128)(2,1)S(1)}, u32[]{:S(2)}, u32[]{:S(2)}) collective-permute-start(bf16[160,4608]{1,0:T(8,128)(2,1)S(1)} %get-tuple-element.20), channel_id=1, source_target_pairs={{0,2},{2,4},{4,6},{6,8},{8,10},{10,12},{12,14},{14,16},{16,18},{18... | collective-permute-start | bytes 4423688 | tf_op jit(solution)/shard_map/ppermute | solution.py:262
  105.8 2.4 %collective-permute-start.14 = (bf16[160,4608]{1,0:T(8,128)(2,1)S(1)}, bf16[160,4608]{1,0:T(8,128)(2,1)S(1)}, u32[]{:S(2)}, u32[]{:S(2)}) collective-permute-start(bf16[160,4608]{1,0:T(8,128)(2,1)S(1)} %get-tuple-element.21), channel_id=1, source_target_pairs={{2,0},{4,2},{6,4},{8,6},{10,8},{12,10},{14,12},{16,14},{18,16},{20... | collective-permute-start | bytes 4423688 | tf_op jit(solution)/shard_map/ppermute | solution.py:262
  108.2 8.0 %coded_products.5 = s32[96,2688]{1,0:T(8,128)S(1)} custom-call(s32[360]{0:T(512)S(1)} %reshape.8.index_ref, bf16[96,4608]{1,0:T(8,128)(2,1)S(1)} %collective-permute-done.3.refs_0_, bf16[96,5120]{1,0:T(8,128)(2,1)S(1)} %collective-permute-done.2.refs_1_, bf16[96,4608]{1,0:T(8,128)(2,1)S(1)} %collective-permute-done.4.refs_2_, bf16[40,9,128,128]{3,2,1,0:T(8,128)(2,1)} %refs_3_.9), custom_call_target="tpu_custom_call" | custom-call | flops 1 | bytes 1 | tf_op jit(solution)/shard_map/coded_products/pallas_call | solution.py:117
  117.3 8.6 %final_products.2.refs_6_ = bf16[256,5120]{1,0:T(8,128)(2,1)} custom-call(s32[360]{0:T(512)S(1)} %reshape.8.index_ref, bf16[96,4608]{1,0:T(8,128)(2,1)} %collective-permute-done.refs_0_, bf16[256,5120]{1,0:T(8,128)(2,1)S(1)} %copy-done, bf16[96,4608]{1,0:T(8,128)(2,1)} %collective-permute-done.1.refs_2_, bf16[40,9,128,128]{3,2,1,0:T(8,128)(2,1)} %refs_3_.9, ...), custom_call_target="tpu_custom_call" | custom-call | flops 1 | bytes 1 | tf_op jit(solution)/shard_map/final_products/pallas_call | solution.py:207
  126.0 11.9 %collective-permute-done.13.refs_0_ = bf16[160,4608]{1,0:T(8,128)(2,1)S(1)} collective-permute-done((bf16[160,4608]{1,0:T(8,128)(2,1)S(1)}, bf16[160,4608]{1,0:T(8,128)(2,1)S(1)}, u32[]{:S(2)}, u32[]{:S(2)}) %collective-permute-start.13) | collective-permute-done | bytes 1474592 | tf_op jit(solution)/shard_map/ppermute | solution.py:262
  137.8 2.8 %collective-permute-done.15.refs_5_ = s32[96,2688]{1,0:T(8,128)S(1)} collective-permute-done((s32[96,2688]{1,0:T(8,128)S(1)}, s32[96,2688]{1,0:T(8,128)S(1)}, u32[]{:S(2)}, u32[]{:S(2)}) %collective-permute-start.15) | collective-permute-done | bytes 1032224 | tf_op jit(solution)/shard_map/ppermute | solution.py:265
  140.7 9.2 %final_products.3 = bf16[256,5120]{1,0:T(8,128)(2,1)} custom-call(s32[360]{0:T(512)S(1)} %reshape.8.index_ref, bf16[160,4608]{1,0:T(8,128)(2,1)S(1)} %collective-permute-done.13.refs_0_, bf16[256,5120]{1,0:T(8,128)(2,1)S(1)} %copy-done, bf16[160,4608]{1,0:T(8,128)(2,1)S(1)} %collective-permute-done.14.refs_2_, ...), custom_call_target="tpu_custom_call", output_to_operand_aliasing={{}: (7, {})} | custom-call | flops 1 | bytes 1 | tf_op jit(solution)/shard_map/final_products/pallas_call | solution.py:207
  (31 shorter events, 7.9 us)
Async XLA Ops:
  0.0 12.1 %copy-start = (bf16[256,5120]{1,0:T(8,128)(2,1)S(1)}, bf16[256,5120]{1,0:T(8,128)(2,1)}, u32[]{:S(2)}) copy-start(bf16[256,5120]{1,0:T(8,128)(2,1)} %refs_1_.3) | copy-start | bytes 7864324
  2.2 11.1 %copy-start.1 = (s32[40,9]{0,1:T(8,128)S(1)}, s32[40,9]{0,1:T(8,128)}, u32[]{:S(2)}) copy-start(s32[40,9]{0,1:T(8,128)} %param.6) | copy-start | bytes 4324
  2.2 11.1 %copy-start.2 = (s32[40]{0:T(128)S(1)}, s32[40]{0:T(128)}, u32[]{:S(2)}) copy-start(s32[40]{0:T(128)} %param.7) | copy-start | bytes 484
  2.2 19.4 %collective-permute-start.8 = (bf16[80,5120]{1,0:T(8,128)(2,1)}, bf16[80,5120]{1,0:T(8,128)(2,1)}, u32[]{:S(2)}, u32[]{:S(2)}) collective-permute-start(bf16[80,5120]{1,0:T(8,128)(2,1)} %slice.55), channel_id=1, source_target_pairs={{0,1},{1,0},{2,3},{3,2},{4,5},{5,4},{6,7},{7,6},{8,9},{9,8},{10,11... | collective-permute-start | bytes 2457608 | tf_op jit(solution)/shard_map/ppermute | solution.py:265
  6.2 24.7 %collective-permute-start.1 = (bf16[96,4608]{1,0:T(8,128)(2,1)}, bf16[96,4608]{1,0:T(8,128)(2,1)}, u32[]{:S(2)}, u32[]{:S(2)}) collective-permute-start(bf16[96,4608]{1,0:T(8,128)(2,1)} %get-tuple-element.27), channel_id=1, source_target_pairs={{2,0},{4,2},{6,4},{8,6},{10,8},{12,10},{14,12},{16,14},{18,16},{20... | collective-permute-start | bytes 2654216 | tf_op jit(solution)/shard_map/ppermute | solution.py:262
  9.1 29.4 %collective-permute-start = (bf16[96,4608]{1,0:T(8,128)(2,1)}, bf16[96,4608]{1,0:T(8,128)(2,1)}, u32[]{:S(2)}, u32[]{:S(2)}) collective-permute-start(bf16[96,4608]{1,0:T(8,128)(2,1)} %get-tuple-element.28), channel_id=1, source_target_pairs={{0,2},{2,4},{4,6},{6,8},{8,10},{10,12},{12,14},{14,16},{16,18},{18... | collective-permute-start | bytes 2654216 | tf_op jit(solution)/shard_map/ppermute | solution.py:262
  13.1 26.0 %collective-permute-start.5 = (bf16[80,5120]{1,0:T(8,128)(2,1)}, bf16[80,5120]{1,0:T(8,128)(2,1)S(1)}, u32[]{:S(2)}, u32[]{:S(2)}) collective-permute-start(bf16[80,5120]{1,0:T(8,128)(2,1)} %slice.52), channel_id=1, source_target_pairs={{0,1},{1,0},{2,3},{3,2},{4,5},{5,4},{6,7},{7,6},{8,9},{9,8},{10,11... | collective-permute-start | bytes 2457608 | tf_op jit(solution)/shard_map/ppermute | solution.py:265
  23.1 23.7 %collective-permute-start.10 = (bf16[80,4608]{1,0:T(8,128)(2,1)S(1)}, bf16[80,4608]{1,0:T(8,128)(2,1)S(1)}, u32[]{:S(2)}, u32[]{:S(2)}) collective-permute-start(bf16[80,4608]{1,0:T(8,128)(2,1)S(1)} %get-tuple-element.33), channel_id=1, source_target_pairs={{2,0},{4,2},{6,4},{8,6},{10,8},{12,10},{14,12},{16,14},{18,16},{20... | collective-permute-start | bytes 2211848 | tf_op jit(solution)/shard_map/ppermute | solution.py:262
  27.8 26.4 %collective-permute-start.9 = (bf16[80,4608]{1,0:T(8,128)(2,1)S(1)}, bf16[80,4608]{1,0:T(8,128)(2,1)S(1)}, u32[]{:S(2)}, u32[]{:S(2)}) collective-permute-start(bf16[80,4608]{1,0:T(8,128)(2,1)S(1)} %get-tuple-element.34), channel_id=1, source_target_pairs={{0,2},{2,4},{4,6},{6,8},{8,10},{10,12},{12,14},{14,16},{16,18},{18... | collective-permute-start | bytes 2211848 | tf_op jit(solution)/shard_map/ppermute | solution.py:262
  38.6 24.4 %collective-permute-start.2 = (bf16[96,5120]{1,0:T(8,128)(2,1)S(1)}, bf16[96,5120]{1,0:T(8,128)(2,1)S(1)}, u32[]{:S(2)}, u32[]{:S(2)}) collective-permute-start(bf16[96,5120]{1,0:T(8,128)(2,1)S(1)} %slice.49), channel_id=1, source_target_pairs={{0,1},{1,0},{2,3},{3,2},{4,5},{5,4},{6,7},{7,6},{8,9},{9,8},{10,11... | collective-permute-start | bytes 2949128 | tf_op jit(solution)/shard_map/ppermute | solution.py:265
  39.2 30.6 %collective-permute-start.7 = (bf16[80,4608]{1,0:T(8,128)(2,1)S(1)}, bf16[80,4608]{1,0:T(8,128)(2,1)S(1)}, u32[]{:S(2)}, u32[]{:S(2)}) collective-permute-start(bf16[80,4608]{1,0:T(8,128)(2,1)S(1)} %get-tuple-element.35), channel_id=1, source_target_pairs={{2,0},{4,2},{6,4},{8,6},{10,8},{12,10},{14,12},{16,14},{18,16},{20... | collective-permute-start | bytes 2211848 | tf_op jit(solution)/shard_map/ppermute | solution.py:262
  42.7 27.1 %collective-permute-start.6 = (bf16[80,4608]{1,0:T(8,128)(2,1)S(1)}, bf16[80,4608]{1,0:T(8,128)(2,1)S(1)}, u32[]{:S(2)}, u32[]{:S(2)}) collective-permute-start(bf16[80,4608]{1,0:T(8,128)(2,1)S(1)} %get-tuple-element.36), channel_id=1, source_target_pairs={{0,2},{2,4},{4,6},{6,8},{8,10},{10,12},{12,14},{14,16},{16,18},{18... | collective-permute-start | bytes 2211848 | tf_op jit(solution)/shard_map/ppermute | solution.py:262
  62.7 17.2 %collective-permute-start.11 = (s32[80,2688]{1,0:T(8,128)S(1)}, s32[80,2688]{1,0:T(8,128)S(1)}, u32[]{:S(2)}, u32[]{:S(2)}) collective-permute-start(s32[80,2688]{1,0:T(8,128)S(1)} %coded_products.4), channel_id=1, source_target_pairs={{0,1},{1,0},{2,3},{3,2},{4,5},{5,4},{6,7},{7,6},{8,9},{9,8},{10,11... | collective-permute-start | bytes 2580488 | tf_op jit(solution)/shard_map/ppermute | solution.py:265
  63.1 40.7 %collective-permute-start.4 = (bf16[96,4608]{1,0:T(8,128)(2,1)S(1)}, bf16[96,4608]{1,0:T(8,128)(2,1)S(1)}, u32[]{:S(2)}, u32[]{:S(2)}) collective-permute-start(bf16[96,4608]{1,0:T(8,128)(2,1)S(1)} %get-tuple-element.31), channel_id=1, source_target_pairs={{2,0},{4,2},{6,4},{8,6},{10,8},{12,10},{14,12},{16,14},{18,16},{20... | collective-permute-start | bytes 2654216 | tf_op jit(solution)/shard_map/ppermute | solution.py:262
  65.0 38.8 %collective-permute-start.3 = (bf16[96,4608]{1,0:T(8,128)(2,1)S(1)}, bf16[96,4608]{1,0:T(8,128)(2,1)S(1)}, u32[]{:S(2)}, u32[]{:S(2)}) collective-permute-start(bf16[96,4608]{1,0:T(8,128)(2,1)S(1)} %get-tuple-element.32), channel_id=1, source_target_pairs={{0,2},{2,4},{4,6},{6,8},{8,10},{10,12},{12,14},{14,16},{16,18},{18... | collective-permute-start | bytes 2654216 | tf_op jit(solution)/shard_map/ppermute | solution.py:262
  79.9 36.3 %collective-permute-start.12 = (s32[80,2688]{1,0:T(8,128)S(1)}, s32[80,2688]{1,0:T(8,128)S(1)}, u32[]{:S(2)}, u32[]{:S(2)}) collective-permute-start(s32[80,2688]{1,0:T(8,128)S(1)} %coded_products.3), channel_id=1, source_target_pairs={{0,1},{1,0},{2,3},{3,2},{4,5},{5,4},{6,7},{7,6},{8,9},{9,8},{10,11... | collective-permute-start | bytes 2580488 | tf_op jit(solution)/shard_map/ppermute | solution.py:265
  103.8 34.0 %collective-permute-start.13 = (bf16[160,4608]{1,0:T(8,128)(2,1)S(1)}, bf16[160,4608]{1,0:T(8,128)(2,1)S(1)}, u32[]{:S(2)}, u32[]{:S(2)}) collective-permute-start(bf16[160,4608]{1,0:T(8,128)(2,1)S(1)} %get-tuple-element.20), channel_id=1, source_target_pairs={{0,2},{2,4},{4,6},{6,8},{8,10},{10,12},{12,14},{14,16},{16,18},{18... | collective-permute-start | bytes 4423688 | tf_op jit(solution)/shard_map/ppermute | solution.py:262
  105.8 32.1 %collective-permute-start.14 = (bf16[160,4608]{1,0:T(8,128)(2,1)S(1)}, bf16[160,4608]{1,0:T(8,128)(2,1)S(1)}, u32[]{:S(2)}, u32[]{:S(2)}) collective-permute-start(bf16[160,4608]{1,0:T(8,128)(2,1)S(1)} %get-tuple-element.21), channel_id=1, source_target_pairs={{2,0},{4,2},{6,4},{8,6},{10,8},{12,10},{14,12},{16,14},{18,16},{20... | collective-permute-start | bytes 4423688 | tf_op jit(solution)/shard_map/ppermute | solution.py:262
  116.2 24.5 %collective-permute-start.15 = (s32[96,2688]{1,0:T(8,128)S(1)}, s32[96,2688]{1,0:T(8,128)S(1)}, u32[]{:S(2)}, u32[]{:S(2)}) collective-permute-start(s32[96,2688]{1,0:T(8,128)S(1)} %coded_products.5), channel_id=1, source_target_pairs={{0,1},{1,0},{2,3},{3,2},{4,5},{5,4},{6,7},{7,6},{8,9},{9,8},{10,11... | collective-permute-start | bytes 3096584 | tf_op jit(solution)/shard_map/ppermute | solution.py:265

commit v2 on v0

--- a/solution.py
+++ b/solution.py
@@ -210,8 +210,8 @@
     reach = W * block
     basis_size, state_size = lax.axis_size("basis"), lax.axis_size("state")
     if states % 256 == 0:
-        sizes = (5 * states // 16, 5 * states // 16, 3 * states // 8)
-        own_sizes = (3 * states // 8, 5 * states // 8)
+        sizes = (5 * states // 16, 3 * states // 8, 5 * states // 16)
+        own_sizes = (7 * states // 16, 9 * states // 16)
     else:
         sizes, own_sizes = (states,), (states,)
     starts, own_starts = starts_of(sizes), starts_of(own_sizes)

time: 137 us -> 137 us (level)
  waiting for transfers between devices: 42.6 us -> 34.3 us
  starting transfers between devices: 37.6 us -> 45.9 us
    ppermute x5, waiting for transfers between devices: 14.9 us -> 2.52 us  [halo(): lax.ppermute(edges[0], 'basis', up)]
    ppermute x5, waiting for transfers between devices: 17.4 us -> 24.1 us  [halo(): lax.ppermute(edges[1], 'basis', down)]
    ppermute x5, starting transfers between devices: 18.7 us -> 25.3 us  [halo(): lax.ppermute(edges[0], 'basis', up)]
    ppermute x6, waiting for transfers between devices: 10.2 us -> 7.75 us  [shifted(): lax.ppermute(piece, 'state', [(i, (i + shift) % state_size) for i in rang...]
    ppermute x6, starting transfers between devices: 4.13 us -> 5.91 us  [shifted(): lax.ppermute(piece, 'state', [(i, (i + shift) % state_size) for i in rang...]
  transfers between devices with their start and end apart: 16 -> 16, of which waited for: 7 -> 5; matrix products, arithmetic and copies ran while one was open for 4% -> 5% of each run, Pallas kernels for 34% -> 34%
where the time goes in v2:
time: 137 us
  Pallas kernels  47.9 us (35%)
  starting transfers between devices  45.9 us (34%)
  waiting for transfers between devices  34.3 us (25%)
  local copies, waits for them, and re-layouts  8.55 us (6%)
    pallas_call x5, Pallas kernels, products(): pl.pallas_call(functools.partial(products_kernel, plan, group, slots, blo...  42.1 us
    ppermute x5, starting transfers between devices, halo(): lax.ppermute(edges[0], 'basis', up)  25.3 us
    ppermute x5, waiting for transfers between devices, halo(): lax.ppermute(edges[1], 'basis', down)  24.1 us
    ppermute x5, starting transfers between devices, halo(): lax.ppermute(edges[1], 'basis', down)  14.6 us
    ppermute x6, waiting for transfers between devices, shifted(): lax.ppermute(piece, 'state', [(i, (i + shift) % state_size) for i in rang...  7.75 us
    ppermute x6, starting transfers between devices, shifted(): lax.ppermute(piece, 'state', [(i, (i + shift) % state_size) for i in rang...  5.91 us
    pallas_call x4, Pallas kernels, finish(): pl.pallas_call(functools.partial(finish_kernel, len(coded), block, pairs)...  5.77 us
    slice x5, local copies, waits for them, and re-layouts, edges_of(): edges = (piece[:, width - reach:], piece[:, :reach])  4.94 us
  transfers between devices with their start and end apart: 16, of which 5 were waited for; matrix products, arithmetic and copies ran while one was open for 5% of the time, Pallas kernels for 34%

profile of v2, /device:TPU:9, one launch (start us, length us, event | category | flops | bytes accessed | tf_op | source)
XLA Modules:
  0.0 137.0 jit_solution(9043705031586844165)
XLA Ops:
  0.0 2.3 %slice.55 = bf16[80,5120]{1,0:T(8,128)(2,1)} slice(bf16[256,5120]{1,0:T(8,128)(2,1)} %refs_1_.3), slice={[0:80], [0:5120]} | slice | bytes 1638400 | tf_op jit(solution)/shard_map/slice | solution.py:253
  3.5 3.0 %fusion = (bf16[112,4608]{1,0:T(8,128)(2,1)}, bf16[112,4608]{1,0:T(8,128)(2,1)}) fusion(bf16[256,5120]{1,0:T(8,128)(2,1)} %refs_1_.3), kind=kLoop, calls=%fused_computation.2 | loop fusion | bytes 4128768 | tf_op jit(solution)/shard_map/slice | solution.py:228
  6.5 2.9 %collective-permute-start.1 = (bf16[112,4608]{1,0:T(8,128)(2,1)}, bf16[112,4608]{1,0:T(8,128)(2,1)}, u32[]{:S(2)}, u32[]{:S(2)}) collective-permute-start(bf16[112,4608]{1,0:T(8,128)(2,1)} %get-tuple-element.27), channel_id=1, source_target_pairs={{2,0},{4,2},{6,4},{8,6},{10,8},{12,10},{14,12},{16,14},{18,16},{20... | collective-permute-start | bytes 3096584 | tf_op jit(solution)/shard_map/ppermute | solution.py:232
  9.4 3.0 %collective-permute-start = (bf16[112,4608]{1,0:T(8,128)(2,1)}, bf16[112,4608]{1,0:T(8,128)(2,1)}, u32[]{:S(2)}, u32[]{:S(2)}) collective-permute-start(bf16[112,4608]{1,0:T(8,128)(2,1)} %get-tuple-element.28), channel_id=1, source_target_pairs={{0,2},{2,4},{4,6},{6,8},{8,10},{10,12},{12,14},{14,16},{16,18},{18... | collective-permute-start | bytes 3096584 | tf_op jit(solution)/shard_map/ppermute | solution.py:232
  14.0 7.7 %collective-permute-done.6.refs_1_ = bf16[80,5120]{1,0:T(8,128)(2,1)S(1)} collective-permute-done((bf16[80,5120]{1,0:T(8,128)(2,1)}, bf16[80,5120]{1,0:T(8,128)(2,1)S(1)}, u32[]{:S(2)}, u32[]{:S(2)}) %collective-permute-start.6) | collective-permute-done | bytes 819232 | tf_op jit(solution)/shard_map/ppermute | solution.py:235
  21.8 4.5 %collective-permute-start.8 = (bf16[80,4608]{1,0:T(8,128)(2,1)S(1)}, bf16[80,4608]{1,0:T(8,128)(2,1)S(1)}, u32[]{:S(2)}, u32[]{:S(2)}) collective-permute-start(bf16[80,4608]{1,0:T(8,128)(2,1)S(1)} %get-tuple-element.33), channel_id=1, source_target_pairs={{2,0},{4,2},{6,4},{8,6},{10,8},{12,10},{14,12},{16,14},{18,16},{20... | collective-permute-start | bytes 2211848 | tf_op jit(solution)/shard_map/ppermute | solution.py:232
  26.3 3.0 %collective-permute-start.7 = (bf16[80,4608]{1,0:T(8,128)(2,1)S(1)}, bf16[80,4608]{1,0:T(8,128)(2,1)S(1)}, u32[]{:S(2)}, u32[]{:S(2)}) collective-permute-start(bf16[80,4608]{1,0:T(8,128)(2,1)S(1)} %get-tuple-element.34), channel_id=1, source_target_pairs={{0,2},{2,4},{4,6},{6,8},{8,10},{10,12},{12,14},{14,16},{16,18},{18... | collective-permute-start | bytes 2211848 | tf_op jit(solution)/shard_map/ppermute | solution.py:232
  29.4 13.0 %collective-permute-done.1.refs_2_ = bf16[112,4608]{1,0:T(8,128)(2,1)} collective-permute-done((bf16[112,4608]{1,0:T(8,128)(2,1)}, bf16[112,4608]{1,0:T(8,128)(2,1)}, u32[]{:S(2)}, u32[]{:S(2)}) %collective-permute-start.1) | collective-permute-done | bytes 1032224 | tf_op jit(solution)/shard_map/ppermute | solution.py:232
  42.8 1.6 %fusion.2 = (bf16[96,4608]{1,0:T(8,128)(2,1)S(1)}, bf16[96,4608]{1,0:T(8,128)(2,1)S(1)}) fusion(bf16[96,5120]{1,0:T(8,128)(2,1)} %collective-permute-done.3.refs_1_), kind=kLoop, calls=%fused_computation.4 | loop fusion | bytes 3538944 | tf_op jit(solution)/shard_map/slice | solution.py:228
  44.4 3.5 %collective-permute-start.5 = (bf16[96,4608]{1,0:T(8,128)(2,1)S(1)}, bf16[96,4608]{1,0:T(8,128)(2,1)S(1)}, u32[]{:S(2)}, u32[]{:S(2)}) collective-permute-start(bf16[96,4608]{1,0:T(8,128)(2,1)S(1)} %get-tuple-element.31), channel_id=1, source_target_pairs={{2,0},{4,2},{6,4},{8,6},{10,8},{12,10},{14,12},{16,14},{18,16},{20... | collective-permute-start | bytes 2654216 | tf_op jit(solution)/shard_map/ppermute | solution.py:232
  47.8 4.2 %collective-permute-start.4 = (bf16[96,4608]{1,0:T(8,128)(2,1)S(1)}, bf16[96,4608]{1,0:T(8,128)(2,1)S(1)}, u32[]{:S(2)}, u32[]{:S(2)}) collective-permute-start(bf16[96,4608]{1,0:T(8,128)(2,1)S(1)} %get-tuple-element.32), channel_id=1, source_target_pairs={{0,2},{2,4},{4,6},{6,8},{8,10},{10,12},{12,14},{14,16},{16,18},{18... | collective-permute-start | bytes 2654216 | tf_op jit(solution)/shard_map/ppermute | solution.py:232
  52.1 8.3 %products.6 = s32[80,2688]{1,0:T(8,128)S(1)} custom-call(s32[360]{0:T(512)S(1)} %reshape.8.index_ref, bf16[80,4608]{1,0:T(8,128)(2,1)S(1)} %collective-permute-done.7.refs_0_, bf16[80,5120]{1,0:T(8,128)(2,1)S(1)} %collective-permute-done.6.refs_1_, bf16[80,4608]{1,0:T(8,128)(2,1)S(1)} %collective-permute-done.8.refs_2_, bf16[40,9,128,128]{3,2,1,0:T(8,128)(2,1)} %refs_3_.9), custom_call_target="tpu_custom_call" | custom-call | flops 1 | bytes 1 | tf_op jit(solution)/shard_map/products/pallas_call | solution.py:136
  61.8 1.9 %collective-permute-start.11 = (bf16[80,4608]{1,0:T(8,128)(2,1)S(1)}, bf16[80,4608]{1,0:T(8,128)(2,1)S(1)}, u32[]{:S(2)}, u32[]{:S(2)}) collective-permute-start(bf16[80,4608]{1,0:T(8,128)(2,1)S(1)} %get-tuple-element.35), channel_id=1, source_target_pairs={{2,0},{4,2},{6,4},{8,6},{10,8},{12,10},{14,12},{16,14},{18,16},{20... | collective-permute-start | bytes 2211848 | tf_op jit(solution)/shard_map/ppermute | solution.py:232
  63.7 10.4 %collective-permute-start.10 = (bf16[80,4608]{1,0:T(8,128)(2,1)S(1)}, bf16[80,4608]{1,0:T(8,128)(2,1)S(1)}, u32[]{:S(2)}, u32[]{:S(2)}) collective-permute-start(bf16[80,4608]{1,0:T(8,128)(2,1)S(1)} %get-tuple-element.36), channel_id=1, source_target_pairs={{0,2},{2,4},{4,6},{6,8},{8,10},{10,12},{12,14},{14,16},{16,18},{18... | collective-permute-start | bytes 2211848 | tf_op jit(solution)/shard_map/ppermute | solution.py:232
  74.1 2.5 %collective-permute-done.4.refs_0_ = bf16[96,4608]{1,0:T(8,128)(2,1)S(1)} collective-permute-done((bf16[96,4608]{1,0:T(8,128)(2,1)S(1)}, bf16[96,4608]{1,0:T(8,128)(2,1)S(1)}, u32[]{:S(2)}, u32[]{:S(2)}) %collective-permute-start.4) | collective-permute-done | bytes 884768 | tf_op jit(solution)/shard_map/ppermute | solution.py:232
  76.6 8.2 %products.5 = s32[96,2688]{1,0:T(8,128)S(1)} custom-call(s32[360]{0:T(512)S(1)} %reshape.8.index_ref, bf16[96,4608]{1,0:T(8,128)(2,1)S(1)} %collective-permute-done.4.refs_0_, bf16[96,5120]{1,0:T(8,128)(2,1)} %collective-permute-done.3.refs_1_, bf16[96,4608]{1,0:T(8,128)(2,1)S(1)} %collective-permute-done.5.refs_2_, bf16[40,9,128,128]{3,2,1,0:T(8,128)(2,1)} %refs_3_.9), custom_call_target="tpu_custom_call" | custom-call | flops 1 | bytes 1 | tf_op jit(solution)/shard_map/products/pallas_call | solution.py:136
  86.0 4.7 %collective-permute-start.13 = (bf16[144,4608]{1,0:T(8,128)(2,1)S(1)}, bf16[144,4608]{1,0:T(8,128)(2,1)S(1)}, u32[]{:S(2)}, u32[]{:S(2)}) collective-permute-start(bf16[144,4608]{1,0:T(8,128)(2,1)S(1)} %get-tuple-element.20), channel_id=1, source_target_pairs={{0,2},{2,4},{4,6},{6,8},{8,10},{10,12},{12,14},{14,16},{16,18},{18... | collective-permute-start | bytes 3981320 | tf_op jit(solution)/shard_map/ppermute | solution.py:232
  90.7 1.9 %collective-permute-start.14 = (bf16[144,4608]{1,0:T(8,128)(2,1)S(1)}, bf16[144,4608]{1,0:T(8,128)(2,1)S(1)}, u32[]{:S(2)}, u32[]{:S(2)}) collective-permute-start(bf16[144,4608]{1,0:T(8,128)(2,1)S(1)} %get-tuple-element.21), channel_id=1, source_target_pairs={{2,0},{4,2},{6,4},{8,6},{10,8},{12,10},{14,12},{16,14},{18,16},{20... | collective-permute-start | bytes 3981320 | tf_op jit(solution)/shard_map/ppermute | solution.py:232
  92.6 11.1 %collective-permute-done.11.refs_2_ = bf16[80,4608]{1,0:T(8,128)(2,1)S(1)} collective-permute-done((bf16[80,4608]{1,0:T(8,128)(2,1)S(1)}, bf16[80,4608]{1,0:T(8,128)(2,1)S(1)}, u32[]{:S(2)}, u32[]{:S(2)}) %collective-permute-start.11) | collective-permute-done | bytes 737312 | tf_op jit(solution)/shard_map/ppermute | solution.py:232
  103.7 8.3 %products.7 = s32[80,2688]{1,0:T(8,128)S(1)} custom-call(s32[360]{0:T(512)S(1)} %reshape.8.index_ref, bf16[80,4608]{1,0:T(8,128)(2,1)S(1)} %collective-permute-done.10.refs_0_, bf16[80,5120]{1,0:T(8,128)(2,1)S(1)} %collective-permute-done.2.refs_1_, bf16[80,4608]{1,0:T(8,128)(2,1)S(1)} %collective-permute-done.11.refs_2_, bf16[40,9,128,128]{3,2,1,0:T(8,128)(2,1)} %refs_3_.9), custom_call_target="tpu_custom_call" | custom-call | flops 1 | bytes 1 | tf_op jit(solution)/shard_map/products/pallas_call | solution.py:136
  112.0 1.8 %collective-permute-start.15 = (s32[80,2688]{1,0:T(8,128)S(1)}, s32[80,2688]{1,0:T(8,128)S(1)}, u32[]{:S(2)}, u32[]{:S(2)}) collective-permute-start(s32[80,2688]{1,0:T(8,128)S(1)} %products.7), channel_id=1, source_target_pairs={{0,1},{1,0},{2,3},{3,2},{4,5},{5,4},{6,7},{7,6},{8,9},{9,8},{10,11... | collective-permute-start | bytes 2580488 | tf_op jit(solution)/shard_map/ppermute | solution.py:235
  113.8 9.9 %products.8.own_ref = f32[112,5120]{1,0:T(8,128)S(1)} custom-call(s32[360]{0:T(512)S(1)} %reshape.8.index_ref, bf16[112,4608]{1,0:T(8,128)(2,1)} %collective-permute-done.refs_0_, bf16[256,5120]{1,0:T(8,128)(2,1)S(1)} %copy-done, bf16[112,4608]{1,0:T(8,128)(2,1)} %collective-permute-done.1.refs_2_, bf16[40,9,128,128]{3,2,1,0:T(8,128)(2,1)} %refs_3_.9), custom_call_target="tpu_custom_call" | custom-call | flops 1 | bytes 1 | tf_op jit(solution)/shard_map/products/pallas_call | solution.py:136
  123.7 1.6 %finish.4.refs_2_ = bf16[256,5120]{1,0:T(8,128)(2,1)} custom-call(f32[112,5120]{1,0:T(8,128)S(1)} %products.8.own_ref, s32[80,2688]{1,0:T(8,128)S(1)} %collective-permute-done.9.refs_0_.refs_1_, s32[80,2688]{1,0:T(8,128)S(1)} %collective-permute-done.9.refs_0_.refs_1_), custom_call_target="tpu_custom_call" | custom-call | flops 1 | bytes 1 | tf_op jit(solution)/shard_map/finish/pallas_call | solution.py:190
  126.4 7.5 %products.9.own_ref = f32[144,5120]{1,0:T(8,128)S(1)} custom-call(s32[360]{0:T(512)S(1)} %reshape.8.index_ref, bf16[144,4608]{1,0:T(8,128)(2,1)S(1)} %collective-permute-done.13.refs_0_, bf16[256,5120]{1,0:T(8,128)(2,1)S(1)} %copy-done, bf16[144,4608]{1,0:T(8,128)(2,1)S(1)} %collective-permute-done.14.refs_2_, bf16[40,9,128,128]{3,2,1,0:T(8,128)(2,1)} %refs_3_.9), custom_call_target="tpu_custom_call" | custom-call | flops 1 | bytes 1 | tf_op jit(solution)/shard_map/products/pallas_call | solution.py:136
  (35 shorter events, 10.1 us)
Async XLA Ops:
  0.0 12.4 %copy-start = (bf16[256,5120]{1,0:T(8,128)(2,1)S(1)}, bf16[256,5120]{1,0:T(8,128)(2,1)}, u32[]{:S(2)}) copy-start(bf16[256,5120]{1,0:T(8,128)(2,1)} %refs_1_.3) | copy-start | bytes 7864324
  2.3 11.5 %copy-start.1 = (s32[40,9]{0,1:T(8,128)S(1)}, s32[40,9]{0,1:T(8,128)}, u32[]{:S(2)}) copy-start(s32[40,9]{0,1:T(8,128)} %param.6) | copy-start | bytes 4324
  2.3 11.5 %copy-start.2 = (s32[40]{0:T(128)S(1)}, s32[40]{0:T(128)}, u32[]{:S(2)}) copy-start(s32[40]{0:T(128)} %param.7) | copy-start | bytes 484
  2.3 19.4 %collective-permute-start.6 = (bf16[80,5120]{1,0:T(8,128)(2,1)}, bf16[80,5120]{1,0:T(8,128)(2,1)S(1)}, u32[]{:S(2)}, u32[]{:S(2)}) collective-permute-start(bf16[80,5120]{1,0:T(8,128)(2,1)} %slice.55), channel_id=1, source_target_pairs={{0,1},{1,0},{2,3},{3,2},{4,5},{5,4},{6,7},{7,6},{8,9},{9,8},{10,11... | collective-permute-start | bytes 2457608 | tf_op jit(solution)/shard_map/ppermute | solution.py:235
  6.5 35.8 %collective-permute-start.1 = (bf16[112,4608]{1,0:T(8,128)(2,1)}, bf16[112,4608]{1,0:T(8,128)(2,1)}, u32[]{:S(2)}, u32[]{:S(2)}) collective-permute-start(bf16[112,4608]{1,0:T(8,128)(2,1)} %get-tuple-element.27), channel_id=1, source_target_pairs={{2,0},{4,2},{6,4},{8,6},{10,8},{12,10},{14,12},{16,14},{18,16},{20... | collective-permute-start | bytes 3096584 | tf_op jit(solution)/shard_map/ppermute | solution.py:232
  9.4 33.0 %collective-permute-start = (bf16[112,4608]{1,0:T(8,128)(2,1)}, bf16[112,4608]{1,0:T(8,128)(2,1)}, u32[]{:S(2)}, u32[]{:S(2)}) collective-permute-start(bf16[112,4608]{1,0:T(8,128)(2,1)} %get-tuple-element.28), channel_id=1, source_target_pairs={{0,2},{2,4},{4,6},{6,8},{8,10},{10,12},{12,14},{14,16},{16,18},{18... | collective-permute-start | bytes 3096584 | tf_op jit(solution)/shard_map/ppermute | solution.py:232
  13.5 29.3 %collective-permute-start.3 = (bf16[96,5120]{1,0:T(8,128)(2,1)}, bf16[96,5120]{1,0:T(8,128)(2,1)}, u32[]{:S(2)}, u32[]{:S(2)}) collective-permute-start(bf16[96,5120]{1,0:T(8,128)(2,1)} %slice.52), channel_id=1, source_target_pairs={{0,1},{1,0},{2,3},{3,2},{4,5},{5,4},{6,7},{7,6},{8,9},{9,8},{10,11... | collective-permute-start | bytes 2949128 | tf_op jit(solution)/shard_map/ppermute | solution.py:235
  21.8 30.2 %collective-permute-start.8 = (bf16[80,4608]{1,0:T(8,128)(2,1)S(1)}, bf16[80,4608]{1,0:T(8,128)(2,1)S(1)}, u32[]{:S(2)}, u32[]{:S(2)}) collective-permute-start(bf16[80,4608]{1,0:T(8,128)(2,1)S(1)} %get-tuple-element.33), channel_id=1, source_target_pairs={{2,0},{4,2},{6,4},{8,6},{10,8},{12,10},{14,12},{16,14},{18,16},{20... | collective-permute-start | bytes 2211848 | tf_op jit(solution)/shard_map/ppermute | solution.py:232
  26.3 25.7 %collective-permute-start.7 = (bf16[80,4608]{1,0:T(8,128)(2,1)S(1)}, bf16[80,4608]{1,0:T(8,128)(2,1)S(1)}, u32[]{:S(2)}, u32[]{:S(2)}) collective-permute-start(bf16[80,4608]{1,0:T(8,128)(2,1)S(1)} %get-tuple-element.34), channel_id=1, source_target_pairs={{0,2},{2,4},{4,6},{6,8},{8,10},{10,12},{12,14},{14,16},{16,18},{18... | collective-permute-start | bytes 2211848 | tf_op jit(solution)/shard_map/ppermute | solution.py:232
  42.4 19.3 %collective-permute-start.2 = (bf16[80,5120]{1,0:T(8,128)(2,1)S(1)}, bf16[80,5120]{1,0:T(8,128)(2,1)S(1)}, u32[]{:S(2)}, u32[]{:S(2)}) collective-permute-start(bf16[80,5120]{1,0:T(8,128)(2,1)S(1)} %slice.49), channel_id=1, source_target_pairs={{0,1},{1,0},{2,3},{3,2},{4,5},{5,4},{6,7},{7,6},{8,9},{9,8},{10,11... | collective-permute-start | bytes 2457608 | tf_op jit(solution)/shard_map/ppermute | solution.py:235
  44.4 29.7 %collective-permute-start.5 = (bf16[96,4608]{1,0:T(8,128)(2,1)S(1)}, bf16[96,4608]{1,0:T(8,128)(2,1)S(1)}, u32[]{:S(2)}, u32[]{:S(2)}) collective-permute-start(bf16[96,4608]{1,0:T(8,128)(2,1)S(1)} %get-tuple-element.31), channel_id=1, source_target_pairs={{2,0},{4,2},{6,4},{8,6},{10,8},{12,10},{14,12},{16,14},{18,16},{20... | collective-permute-start | bytes 2654216 | tf_op jit(solution)/shard_map/ppermute | solution.py:232
  47.8 28.8 %collective-permute-start.4 = (bf16[96,4608]{1,0:T(8,128)(2,1)S(1)}, bf16[96,4608]{1,0:T(8,128)(2,1)S(1)}, u32[]{:S(2)}, u32[]{:S(2)}) collective-permute-start(bf16[96,4608]{1,0:T(8,128)(2,1)S(1)} %get-tuple-element.32), channel_id=1, source_target_pairs={{0,2},{2,4},{4,6},{6,8},{8,10},{10,12},{12,14},{14,16},{16,18},{18... | collective-permute-start | bytes 2654216 | tf_op jit(solution)/shard_map/ppermute | solution.py:232
  60.4 24.4 %collective-permute-start.9 = (s32[80,2688]{1,0:T(8,128)S(1)}, s32[80,2688]{1,0:T(8,128)S(1)}, u32[]{:S(2)}, u32[]{:S(2)}) collective-permute-start(s32[80,2688]{1,0:T(8,128)S(1)} %products.6), channel_id=1, source_target_pairs={{0,1},{1,0},{2,3},{3,2},{4,5},{5,4},{6,7},{7,6},{8,9},{9,8},{10,11... | collective-permute-start | bytes 2580488 | tf_op jit(solution)/shard_map/ppermute | solution.py:235
  61.8 41.9 %collective-permute-start.11 = (bf16[80,4608]{1,0:T(8,128)(2,1)S(1)}, bf16[80,4608]{1,0:T(8,128)(2,1)S(1)}, u32[]{:S(2)}, u32[]{:S(2)}) collective-permute-start(bf16[80,4608]{1,0:T(8,128)(2,1)S(1)} %get-tuple-element.35), channel_id=1, source_target_pairs={{2,0},{4,2},{6,4},{8,6},{10,8},{12,10},{14,12},{16,14},{18,16},{20... | collective-permute-start | bytes 2211848 | tf_op jit(solution)/shard_map/ppermute | solution.py:232
  63.7 40.0 %collective-permute-start.10 = (bf16[80,4608]{1,0:T(8,128)(2,1)S(1)}, bf16[80,4608]{1,0:T(8,128)(2,1)S(1)}, u32[]{:S(2)}, u32[]{:S(2)}) collective-permute-start(bf16[80,4608]{1,0:T(8,128)(2,1)S(1)} %get-tuple-element.36), channel_id=1, source_target_pairs={{0,2},{2,4},{4,6},{6,8},{8,10},{10,12},{12,14},{14,16},{16,18},{18... | collective-permute-start | bytes 2211848 | tf_op jit(solution)/shard_map/ppermute | solution.py:232
  84.8 27.2 %collective-permute-start.12 = (s32[96,2688]{1,0:T(8,128)S(1)}, s32[96,2688]{1,0:T(8,128)S(1)}, u32[]{:S(2)}, u32[]{:S(2)}) collective-permute-start(s32[96,2688]{1,0:T(8,128)S(1)} %products.5), channel_id=1, source_target_pairs={{0,1},{1,0},{2,3},{3,2},{4,5},{5,4},{6,7},{7,6},{8,9},{9,8},{10,11... | collective-permute-start | bytes 3096584 | tf_op jit(solution)/shard_map/ppermute | solution.py:235
  86.0 40.5 %collective-permute-start.13 = (bf16[144,4608]{1,0:T(8,128)(2,1)S(1)}, bf16[144,4608]{1,0:T(8,128)(2,1)S(1)}, u32[]{:S(2)}, u32[]{:S(2)}) collective-permute-start(bf16[144,4608]{1,0:T(8,128)(2,1)S(1)} %get-tuple-element.20), channel_id=1, source_target_pairs={{0,2},{2,4},{4,6},{6,8},{8,10},{10,12},{12,14},{14,16},{16,18},{18... | collective-permute-start | bytes 3981320 | tf_op jit(solution)/shard_map/ppermute | solution.py:232
  90.7 35.8 %collective-permute-start.14 = (bf16[144,4608]{1,0:T(8,128)(2,1)S(1)}, bf16[144,4608]{1,0:T(8,128)(2,1)S(1)}, u32[]{:S(2)}, u32[]{:S(2)}) collective-permute-start(bf16[144,4608]{1,0:T(8,128)(2,1)S(1)} %get-tuple-element.21), channel_id=1, source_target_pairs={{2,0},{4,2},{6,4},{8,6},{10,8},{12,10},{14,12},{16,14},{18,16},{20... | collective-permute-start | bytes 3981320 | tf_op jit(solution)/shard_map/ppermute | solution.py:232
  112.0 23.4 %collective-permute-start.15 = (s32[80,2688]{1,0:T(8,128)S(1)}, s32[80,2688]{1,0:T(8,128)S(1)}, u32[]{:S(2)}, u32[]{:S(2)}) collective-permute-start(s32[80,2688]{1,0:T(8,128)S(1)} %products.7), channel_id=1, source_target_pairs={{0,1},{1,0},{2,3},{3,2},{4,5},{5,4},{6,7},{7,6},{8,9},{9,8},{10,11... | collective-permute-start | bytes 2580488 | tf_op jit(solution)/shard_map/ppermute | solution.py:235
